TPU v7x, 512 devices: a whole 4x4x16 slice. The times are simulated.
512 devices in a mesh: seq: 64 (over y, z), tp: 8 (over x, core).
Axes of the slice: x: 4, y: 4, z: 16, core: 2. Of those that a mesh axis runs over, the one named last changes fastest.
Arguments:
- queries: bfloat16 [4096, 8192], P('seq', 'tp'), may hold values from -8 to 8
- keys: bfloat16 [4096, 1024], P('seq', 'tp'), may hold values from -8 to 8
- values: bfloat16 [4096, 1024], P('seq', 'tp'), may hold values from -6 to 6
- segment_ids: int32 [4096], P('seq'), may hold values from 0 to 17, as said below
- out_weight: bfloat16 [8192, 16384], P('tp', 'seq'), may hold values from -0.0625 to 0.0625
Outputs:
- mixed: bfloat16 [4096, 16384], P('tp', 'seq')
Inputs may be any that keep to these rules, and one draw needn't show every extreme that they name: `segment_ids`: document ids start at 0 at the first token, never fall, and rise by at most one from a token to the next; one document covers exactly 2112 tokens.
All inputs are finite; a program needn't handle non-finite values.
Results may differ from a plain program's by a relative error of at most 0.019.
Values may be sent and summed in bfloat16 or wider, within the bound.
No kernel may reach another device: no remote copies, remote signals or barrier semaphores. Data moves between devices by JAX's collectives and lax.ppermute only.
A program may use at most 64 MiB of HBM per device.

v0:
```python
import math

import jax
import jax.numpy as jnp
from jax import lax
from jax.sharding import PartitionSpec as P

HD = 128
GROUP = 8


masked_score = -1e30


def body(queries, keys, values, segment_ids, out_weight):
    seq_rank = lax.axis_index("seq")
    tok_count = queries.shape[0]
    local_heads = keys.shape[1] // HD
    score_scale = 1.0 / math.sqrt(HD)
    all_segments = lax.all_gather(segment_ids, "seq", axis=0, tiled=True)
    offsets = jnp.arange(tok_count, dtype=jnp.int32)
    positions = seq_rank * tok_count + offsets
    query_segments = jnp.take(all_segments, positions)
    grouped = queries.reshape(tok_count, local_heads, GROUP, HD)
    key_block = lax.all_gather(keys, "seq", axis=0, tiled=True)
    value_block = lax.all_gather(values, "seq", axis=0, tiled=True)
    block_rows = key_block.shape[0]
    key_pos = jnp.arange(block_rows, dtype=jnp.int32)
    allowed = (key_pos[None, :] <= positions[:, None]) & (
        all_segments[None, :] == query_segments[:, None]
    )
    running_max = jnp.full((local_heads, tok_count, GROUP), masked_score, jnp.float32)
    key_heads = key_block.reshape(block_rows, local_heads, HD)
    value_heads = value_block.reshape(block_rows, local_heads, HD)
    scores = (
        jnp.einsum("thgd,nhd->htgn", grouped, key_heads, preferred_element_type=jnp.float32)
        * score_scale
    )
    keep_mask = allowed[None, :, None, :]
    new_max = jnp.maximum(running_max, jnp.max(jnp.where(keep_mask, scores, masked_score), axis=-1))
    weights = jnp.where(keep_mask, jnp.exp(scores - new_max[..., None]), 0.0)
    running_sum = jnp.sum(weights, axis=-1)
    summed = jnp.einsum(
        "htgn,nhd->htgd",
        weights.astype(jnp.bfloat16),
        value_heads,
        preferred_element_type=jnp.float32,
    )
    attended = (
        (summed / running_sum[..., None])
        .transpose(1, 0, 2, 3)
        .reshape(tok_count, local_heads * GROUP * HD)
    )
    attended = attended.astype(jnp.bfloat16)
    partial_out = jnp.dot(
        lax.all_gather(attended, "seq", axis=0, tiled=True),
        out_weight,
        preferred_element_type=jnp.float32,
    )
    summed_out = lax.psum_scatter(
        partial_out.astype(jnp.bfloat16), "tp", scatter_dimension=0, tiled=True
    )
    return summed_out


def solution(mesh):
    return jax.shard_map(
        body,
        mesh=mesh,
        in_specs=(P("seq", "tp"), P("seq", "tp"), P("seq", "tp"), P("seq"), P("tp", "seq")),
        out_specs=P("tp", "seq"),
        check_vma=False,
    )
```

profile of v0, /device:TPU:32, one launch (start us, length us, event | category | flops | bytes accessed | tf_op | source)
XLA Modules:
  0.0 510.0 jit_solution(17353476639463040653)
XLA Ops:
  6.5 0.0 copy-start
  6.5 0.0 all-gather.4.cloned.1.call-start
  6.5 0.7 all-gather.4.cloned.1.call-update
  7.3 0.0 all-gather.6.cloned.1.call-start
  7.3 0.7 all-gather.6.cloned.1.call-update
  8.0 0.0 all-gather.8.cloned.1.call-start
  8.1 1.3 dynamic-slice
  10.0 0.9 dynamic-update-slice
  10.9 280.7 %all-reduce = s32[4096]{0:T(1024)S(1)} all-reduce(s32[4096]{0:T(1024)S(1)} %dynamic-update-slice), channel_id=1, replica_groups=mesh['seq'=64,'tp'=8] {'seq'}, use_global_device_ids=true, to_apply=%add | all-reduce | flops 4096 | bytes 32768
  291.7 0.8 gather_fusion
  292.4 0.9 copy.6
  293.4 0.3 fusion.14
  293.6 0.0 all-gather.4.cloned.1.call-done
  293.7 3.5 select_reduce_fusion
  297.2 3.2 copy-done.1
  300.4 2.6 fusion
  303.0 5.6 %fusion.8 = bf16[64,8,128]{2,1,0:T(8,128)(2,1)S(1)} fusion(f32[64,8,4096]{2,1,0:T(8,128)} %copy-done.1, f32[64,8]{1,0:T(8,128)S(1)} %broadcast_maximum_fusion, pred[64,4096]{1,0:T(8,128)(4,1)S(1)} %fusion.14, bf16[4096,128]{1,0:T(8,128)(2,1)} %all-gather.6.cloned.1.call-done, f32[64,8]{1,0:T(8,128)S(1)} %fusion), kind=kOutput, calls=%fused_computation.9 | convolution fusion | flops 545390592 | bytes 9834496 | tf_op jit(solution)/shard_map/htgn,nhd->htgd/dot_general | solution.py:43
  308.6 0.7 copy.9
  309.3 0.0 all-gather.8.cloned.1.call-update
  309.3 0.0 reduce-scatter.2.cloned.1.call-start
  309.3 151.0 %all-gather.8.cloned.1.call-done = bf16[4096,1024]{1,0:T(8,128)(2,1)} async-done(((bf16[64,1024]{1,0:T(8,128)(2,1)}), bf16[4096,1024]{1,0:T(8,128)(2,1)}) %all-gather.8.cloned.1.call-update) | async-done | bytes 8388624 | tf_op jit(solution)/shard_map/all_gather | solution.py:56
  460.3 7.1 %convolution_convert_fusion = bf16[4096,256]{1,0:T(8,128)(2,1)} fusion(bf16[4096,1024]{1,0:T(8,128)(2,1)} %all-gather.8.cloned.1.call-done, bf16[1024,256]{1,0:T(8,128)(2,1)S(1)} %copy-done), kind=kOutput, calls=%fused_computation.5 | convolution fusion | flops 2148532224 | bytes 11010048 | tf_op jit(solution)/shard_map/dot_general | solution.py:55
  467.4 0.0 reduce-scatter.2.cloned.1.call-update
  467.4 36.0 %reduce-scatter.2.cloned.1.call-done = bf16[512,256]{1,0:T(8,128)(2,1)} async-done(((bf16[4096,256]{1,0:T(8,128)(2,1)}), bf16[512,256]{1,0:T(8,128)(2,1)}) %reduce-scatter.2.cloned.1.call-update) | async-done | bytes 262160 | tf_op jit(solution)/shard_map/reduce_scatter | solution.py:60
  (9 shorter events, 0.0 us)
Async XLA Ops:
  6.5 453.8 %copy-start = (bf16[1024,256]{1,0:T(8,128)(2,1)S(1)}, bf16[1024,256]{1,0:T(8,128)(2,1)}, u32[]{:S(2)}) copy-start(bf16[1024,256]{1,0:T(8,128)(2,1)} %param.9) | copy-start | bytes 1572868
  6.5 287.1 %all-gather.4.cloned.1.call-start = ((), (), s32[]{:S(2)}) async-start(), calls=%async_computation.1 | async-start | bytes 1064960 | tf_op jit(solution)/shard_map/all_gather | solution.py:25
  7.3 295.7 %all-gather.6.cloned.1.call-start = ((), (), s32[]{:S(2)}) async-start(), calls=%async_computation.2 | async-start | bytes 1064960 | tf_op jit(solution)/shard_map/all_gather | solution.py:26
  8.0 452.3 %all-gather.8.cloned.1.call-start = ((), (), s32[]{:S(2)}) async-start(), calls=%async_computation.3 | async-start | bytes 8519680 | tf_op jit(solution)/shard_map/all_gather | solution.py:56
  297.1 3.2 copy-start.1
  309.3 194.2 %reduce-scatter.2.cloned.1.call-start = ((), (), s32[]{:S(2)}) async-start(), calls=%async_computation.4 | async-start | bytes 2359296 | tf_op jit(solution)/shard_map/reduce_scatter | solution.py:60
Sparse Core Ops, SparseCore 0:
  10.3 142.1 all-gather.3
  155.4 135.0 all-gather.5
  309.4 150.8 all-gather.7
  467.6 35.8 reduce-scatter.1
where the time goes:
time: 510 us
  blocking collectives  281 us (55%)
  waiting for transfers between devices  188 us (37%)
  matrix products  16.1 us (3%)
  between operations  13.9 us (3%)
  local copies, waits for them, and re-layouts  7.72 us (2%)
    unnamed x1, blocking collectives  281 us
    all_gather x1, waiting for transfers between devices, body(): lax.all_gather(attended, 'seq', axis=0, tiled=True)  151 us
    reduce_scatter x1, waiting for transfers between devices, body(): lax.psum_scatter(partial_out.astype(jnp.bfloat16), 'tp', scatter_dimensio...  36 us
  transfers between devices with their start and end apart: 4, of which 2 were waited for; matrix products, arithmetic and copies ran while one was open for 2% of the time, Pallas kernels for 0%

commit v1 on v0

v1 whole, which is shorter than its diff:
```python
import math

import jax
import jax.numpy as jnp
from jax import lax
from jax.experimental import pallas as pl
from jax.experimental.pallas import tpu as pltpu
from jax.sharding import PartitionSpec as P

HD = 128
GROUP = 8
TOK = 64
NY, NZ, NX, NC = 4, 16, 4, 2
CHUNK = 4 * TOK
CHUNKS = 10
SEG_ROWS = 16
BAND = NZ * TOK + SEG_ROWS
MASKED = -1e30

Y_GROUPS = [[y * NZ + z for y in range(NY)] for z in range(NZ)]
Z_GROUPS = [[y * NZ + z for z in range(NZ)] for y in range(NY)]
X_GROUPS = [[x * NC + c for x in range(NX)] for c in range(NC)]
CORE_SWAP = [(t, t ^ 1) for t in range(NX * NC)]


def flat(y, z, x, c):
    return ((y * NZ + z) * NX + x) * NC + c


XY_SWAP = [
    (flat(y, z, x, c), flat(x, z, y, c))
    for y in range(NY)
    for z in range(NZ)
    for x in range(NX)
    for c in range(NC)
]


def attend(q_ref, seg_ref, kv_ref, ids_ref, out_ref, score_ref):
    rank = lax.axis_index("seq")
    first_chunk = jnp.maximum(rank // 4 - (CHUNKS - 1), 0)
    own = seg_ref[...].astype(jnp.float32)
    rows = lax.broadcasted_iota(jnp.int32, (TOK, TOK), 0)
    cols = lax.broadcasted_iota(jnp.int32, (TOK, TOK), 1)
    across = jnp.broadcast_to(own, (TOK, TOK))
    down = jnp.sum(jnp.where(rows == cols, across, 0.0), axis=1, keepdims=True)
    below = jnp.sum((across < down).astype(jnp.float32), axis=1, keepdims=True)
    head_id = jnp.min(down)
    pairs = ids_ref[...].astype(jnp.float32)
    ids = pairs[:, :TOK] + 128.0 * pairs[:, TOK:]
    block = lax.broadcasted_iota(jnp.int32, ids.shape, 0)
    earlier = jnp.sum(((ids == head_id) & (block < rank)).astype(jnp.float32))
    begin = (rank * TOK).astype(jnp.float32) + jnp.where(down == head_id, -earlier, below)
    begin = begin.astype(jnp.int32)
    position = rank * TOK + lax.broadcasted_iota(jnp.int32, (TOK, 1), 0)

    queries = jnp.concatenate([q_ref[:, g * HD : (g + 1) * HD] for g in range(GROUP)], axis=0)
    best = jnp.full((GROUP * TOK, HD), MASKED, jnp.float32)

    def key_rows(i):
        chunk = first_chunk + i
        return pl.ds(pl.multiple_of(chunk // 4 * BAND + chunk % 4 * CHUNK, 16), CHUNK)

    for i in range(CHUNKS):
        keys = kv_ref[key_rows(i), :HD]
        scores = lax.dot_general(
            queries, keys, (((1,), (1,)), ((), ())), preferred_element_type=jnp.float32
        )
        at = (first_chunk + i) * CHUNK + lax.broadcasted_iota(jnp.int32, (TOK, CHUNK), 1)
        keep = (at >= begin) & (at <= position)
        scores = jnp.where(keep[None], scores.reshape(GROUP, TOK, CHUNK), MASKED)
        scores = scores.reshape(GROUP * TOK, CHUNK)
        score_ref[i] = scores
        best = jnp.maximum(best, jnp.maximum(scores[:, :HD], scores[:, HD:]))
    scale = math.log2(math.e) / math.sqrt(HD)
    top = jnp.max(best, axis=1, keepdims=True) * scale
    total = jnp.zeros((GROUP * TOK, HD), jnp.float32)
    mixed = jnp.zeros((GROUP * TOK, HD), jnp.float32)
    for i in range(CHUNKS):
        weights = jnp.exp2(score_ref[i] * scale - top)
        total += weights[:, :HD] + weights[:, HD:]
        mixed += jnp.dot(
            weights.astype(jnp.bfloat16),
            kv_ref[key_rows(i), HD:],
            preferred_element_type=jnp.float32,
        )
    result = (mixed / jnp.sum(total, axis=1, keepdims=True)).astype(jnp.bfloat16)
    for g in range(GROUP):
        out_ref[:, g * HD : (g + 1) * HD] = result[g * TOK : (g + 1) * TOK]


def body(queries, keys, values, segment_ids, out_weight):
    core = lax.axis_index("tp") % NC
    weight = lax.all_gather(out_weight, "seq", axis_index_groups=Y_GROUPS)

    pair = jnp.concatenate([keys, values], axis=1)
    low, high = segment_ids % 128, segment_ids // 128
    tag = jnp.concatenate([low, high, jnp.zeros_like(low), jnp.zeros_like(low)])[None]
    tag = jnp.pad(tag, ((0, SEG_ROWS - 1), (0, 0))).astype(jnp.bfloat16)
    message = jnp.concatenate([pair, tag], axis=0)
    band = lax.all_gather(message, "seq", axis_index_groups=Z_GROUPS)
    band = jnp.concatenate([band[:, :TOK].reshape(NZ * TOK, 2 * HD), band[:, TOK]], axis=0)
    bands = lax.all_gather(
        band.astype(jnp.float16), "seq", axis_index_groups=Y_GROUPS, tiled=True
    ).astype(jnp.bfloat16)
    ids = bands.reshape(NY, BAND, 2 * HD)[:, NZ * TOK :, :HD].reshape(NY * NZ, HD)

    attended = pl.pallas_call(
        attend,
        out_shape=jax.ShapeDtypeStruct((TOK, GROUP * HD), jnp.bfloat16),
        in_specs=[pl.BlockSpec(memory_space=pltpu.VMEM)] * 4,
        out_specs=pl.BlockSpec(memory_space=pltpu.VMEM),
        scratch_shapes=[pltpu.VMEM((CHUNKS, GROUP * TOK, CHUNK), jnp.float32)],
        compiler_params=pltpu.CompilerParams(vmem_limit_bytes=40 * 1024 * 1024),
        cost_estimate=pl.CostEstimate(
            flops=4 * GROUP * TOK * CHUNKS * CHUNK * HD,
            bytes_accessed=3 * 1024 * 1024,
            transcendentals=GROUP * TOK * CHUNKS * CHUNK,
        ),
    )(queries, segment_ids.reshape(1, TOK), bands, ids)

    rows = lax.all_gather(attended.astype(jnp.float16), "seq", axis_index_groups=Z_GROUPS)
    rows = rows.astype(jnp.bfloat16).reshape(NC, NZ * TOK // NC, GROUP * HD)

    def project(which):
        half = lax.dynamic_index_in_dim(rows, which, 0, keepdims=False)
        return jnp.einsum("rk,ykn->yrn", half, weight, preferred_element_type=jnp.float32)

    theirs = lax.ppermute(project(1 - core).astype(jnp.bfloat16), "tp", CORE_SWAP)
    both = (project(core) + theirs.astype(jnp.float32)).astype(jnp.bfloat16)
    parts = lax.all_to_all(both, "tp", 0, 0, axis_index_groups=X_GROUPS, tiled=True)
    mixed = jnp.sum(parts.astype(jnp.float32), axis=0).astype(jnp.bfloat16)
    return lax.ppermute(mixed, ("seq", "tp"), XY_SWAP)


def solution(mesh):
    return jax.shard_map(
        body,
        mesh=mesh,
        in_specs=(P("seq", "tp"), P("seq", "tp"), P("seq", "tp"), P("seq"), P("tp", "seq")),
        out_specs=P("tp", "seq"),
        check_vma=False,
    )
```

time: 510 us -> 176 us (0.35)
  the two profiles are of different devices: /device:TPU:32 before, /device:TPU:24 now
where the time goes in v1:
time: 176 us; the launch traced here: 175 us
  blocking collectives  124 us (70%)
  waiting for transfers between devices  16.9 us (10%)
  between operations  13.5 us (8%)
  matrix products  6.67 us (4%)
  starting transfers between devices  6.35 us (4%)
  Pallas kernels  3.65 us (2%)
  other arithmetic  2.81 us (2%)
    all_gather x1, blocking collectives, body(): lax.all_gather(attended.astype(jnp.float16), 'seq', axis_index_groups=Z_G...  44.9 us
    all_gather x1, blocking collectives, body(): band = lax.all_gather(message, 'seq', axis_index_groups=Z_GROUPS)  39.2 us
    all_gather x1, blocking collectives, body(): lax.all_gather(band.astype(jnp.float16), 'seq', axis_index_groups=Y_GROUP...  20.4 us
    all_to_all x1, blocking collectives, body(): lax.all_to_all(both, 'tp', 0, 0, axis_index_groups=X_GROUPS, tiled=True)  19.4 us
    ppermute x1, waiting for transfers between devices, body(): return lax.ppermute(mixed, ('seq', 'tp'), XY_SWAP)  13.3 us
    dot_general x2, matrix products, project(): jnp.einsum('rk,ykn->yrn', half, weight, preferred_element_type=jnp.float32)  6.67 us
    ppermute x1, starting transfers between devices, body(): return lax.ppermute(mixed, ('seq', 'tp'), XY_SWAP)  4.44 us
    pallas_call x1, Pallas kernels, body(): pl.pallas_call(attend, out_shape=jax.ShapeDtypeStruct((TOK, GROUP * HD),...  3.65 us
  transfers between devices with their start and end apart: 3, of which 2 were waited for; matrix products, arithmetic and copies ran while one was open for 2% of the time, Pallas kernels for 2%

profile of v1, /device:TPU:24, one launch (start us, length us, event | category | flops | bytes accessed | tf_op | source)
XLA Modules:
  0.0 175.1 jit_solution(10076173425505417458)
XLA Ops:
  6.5 0.0 all-gather.7.cloned.1.call-start
  6.5 0.7 all-gather.7.cloned.1.call-update
  7.3 0.7 fusion.8
  7.9 0.1 pad_maximum_fusion
  8.0 0.7 fusion.7
  8.8 39.2 %all-gather = bf16[1280,256]{1,0:T(8,128)(2,1)S(1)} all-gather(bf16[80,256]{1,0:T(8,128)(2,1)S(1)} %fusion.7), channel_id=2, replica_groups={{0,8,16,24,32,40,48,56,64,72,80,88,96,104,112,120},{128,136,144,152,160..., dimensions={0}, use_global_device_ids=true | all-gather | bytes 696320 | tf_op jit(solution)/shard_map/all_gather | solution.py:101
  48.1 0.1 maximum_convert_fusion
  48.2 20.4 %all-gather.8 = f16[4160,256]{1,0:T(8,128)(2,1)S(1)} all-gather(f16[1040,256]{1,0:T(8,128)(2,1)S(1)} %maximum_convert_fusion), channel_id=1, replica_groups={{0,128,256,384},{8,136,264,392},{16,144,272,400},{24,152,280,408},{32,1..., dimensions={0}, use_global_device_ids=true | all-gather | bytes 2662400 | tf_op jit(solution)/shard_map/all_gather | solution.py:103
  68.6 0.4 convert_element_type.28.kv_ref
  69.0 0.5 copy-done
  69.5 0.0 copy-done.1
  69.5 3.6 %shard_map.55 = bf16[64,1024]{1,0:T(8,128)(2,1)S(1)} custom-call(bf16[64,1024]{1,0:T(8,128)(2,1)S(1)} %copy-done, s32[1,64]{1,0:T(1,128)S(1)} %bitcast.28, bf16[4160,256]{1,0:T(8,128)(2,1)S(1)} %convert_element_type.28.kv_ref, bf16[64,128]{1,0:T(8,128)(2,1)S(1)} %bitcast.27), custom_call_target="tpu_custom_call" | custom-call | flops 671088640 | bytes 3145728 | tf_op jit(solution)/shard_map/pallas_call | solution.py:108
  73.2 44.9 %all-gather.9 = f16[1024,1024]{1,0:T(8,128)(2,1)S(1)} all-gather(f16[64,1024]{1,0:T(8,128)(2,1)S(1)} %convert_element_type.29), channel_id=3, replica_groups={{0,8,16,24,32,40,48,56,64,72,80,88,96,104,112,120},{128,136,144,152,160..., dimensions={0}, use_global_device_ids=true | all-gather | bytes 2228224 | tf_op jit(solution)/shard_map/all_gather | solution.py:122
  118.1 0.6 convert_element_type.35
  118.7 0.0 all-gather.7.cloned.1.call-done
  118.7 3.8 %fusion.1 = bf16[4,512,256]{2,1,0:T(8,128)(2,1)} fusion(bf16[4,1024,256]{2,1,0:T(8,128)(2,1)} %bitcast.35, bf16[2,512,1024]{2,1,0:T(8,128)(2,1)S(1)} %bitcast.31, s32[]{:T(128)S(6)} %select_n.29), kind=kOutput, calls=%fused_computation.3 | convolution fusion | flops 1074266112 | bytes 4194308 | tf_op jit(solution)/shard_map/rk,ykn->yrn/dot_general | solution.py:127
  122.5 1.9 %collective-permute-start = (bf16[4,512,256]{2,1,0:T(8,128)(2,1)}, bf16[4,512,256]{2,1,0:T(8,128)(2,1)S(1)}, u32[]{:S(2)}, u32[]{:S(2)}) collective-permute-start(bf16[4,512,256]{2,1,0:T(8,128)(2,1)} %fusion.1), channel_id=1, source_target_pairs={{0,1},{1,0},{2,3},{3,2},{4,5},{5,4},{6,7},{7,6},{8,9},{9,8},{10,11... | collective-permute-start | bytes 3145736 | tf_op jit(solution)/shard_map/ppermute | solution.py:129
  124.5 2.8 %collective-permute-done = bf16[4,512,256]{2,1,0:T(8,128)(2,1)S(1)} collective-permute-done((bf16[4,512,256]{2,1,0:T(8,128)(2,1)}, bf16[4,512,256]{2,1,0:T(8,128)(2,1)S(1)}, u32[]{:S(2)}, u32[]{:S(2)}) %collective-permute-start) | collective-permute-done | bytes 1048608 | tf_op jit(solution)/shard_map/ppermute | solution.py:129
  127.3 2.8 %fusion = bf16[4,512,256]{2,1,0:T(8,128)(2,1)S(1)} fusion(bf16[4,512,256]{2,1,0:T(8,128)(2,1)S(1)} %collective-permute-done, bf16[4,1024,256]{2,1,0:T(8,128)(2,1)} %bitcast.36, bf16[2,512,1024]{2,1,0:T(8,128)(2,1)S(1)} %bitcast.32, s32[]{:T(128)S(6)} %select_n.28), kind=kOutput, calls=%fused_computation.1 | convolution fusion | flops 1075314688 | bytes 5242884 | tf_op jit(solution)/shard_map/rk,ykn->yrn/dot_general | solution.py:127
  130.1 19.4 %all_to_all.5 = bf16[4,512,256]{2,1,0:T(8,128)(2,1)S(1)} all-to-all(bf16[4,512,256]{2,1,0:T(8,128)(2,1)S(1)} %fusion), channel_id=1, replica_groups={{0,2,4,6},{1,3,5,7},{8,10,12,14},{9,11,13,15},{16,18,20,22},{17,19,21,2..., dimensions={0} | all-to-all | bytes 2097152 | tf_op jit(solution)/shard_map/all_to_all | solution.py:131
  149.6 0.3 reduce_sum.12
  149.8 4.4 %collective-permute-start.1 = (bf16[512,256]{1,0:T(8,128)(2,1)S(1)}, bf16[512,256]{1,0:T(8,128)(2,1)S(1)}, u32[]{:S(2)}, u32[]{:S(2)}) collective-permute-start(bf16[512,256]{1,0:T(8,128)(2,1)S(1)} %reduce_sum.12), channel_id=1, source_target_pairs={{0,0},{1,1},{2,128},{3,129},{4,256},{5,257},{6,384},{7,385},{8,8},... | collective-permute-start | bytes 786440 | tf_op jit(solution)/shard_map/ppermute | solution.py:133
  154.3 13.3 %collective-permute-done.1 = bf16[512,256]{1,0:T(8,128)(2,1)S(1)} collective-permute-done((bf16[512,256]{1,0:T(8,128)(2,1)S(1)}, bf16[512,256]{1,0:T(8,128)(2,1)S(1)}, u32[]{:S(2)}, u32[]{:S(2)}) %collective-permute-start.1) | collective-permute-done | bytes 262176 | tf_op jit(solution)/shard_map/ppermute | solution.py:133
  167.6 0.7 copy.11
  (9 shorter events, 0.1 us)
Async XLA Ops:
  6.5 112.2 %all-gather.7.cloned.1.call-start = ((), (), s32[]{:S(2)}) async-start(), calls=%async_computation.1 | async-start | bytes 2621440 | tf_op jit(solution)/shard_map/all_gather | solution.py:94
  68.6 0.9 copy-start
  68.6 0.9 copy-start.1
  122.5 4.8 %collective-permute-start = (bf16[4,512,256]{2,1,0:T(8,128)(2,1)}, bf16[4,512,256]{2,1,0:T(8,128)(2,1)S(1)}, u32[]{:S(2)}, u32[]{:S(2)}) collective-permute-start(bf16[4,512,256]{2,1,0:T(8,128)(2,1)} %fusion.1), channel_id=1, source_target_pairs={{0,1},{1,0},{2,3},{3,2},{4,5},{5,4},{6,7},{7,6},{8,9},{9,8},{10,11... | collective-permute-start | bytes 3145736 | tf_op jit(solution)/shard_map/ppermute | solution.py:129
  149.8 17.7 %collective-permute-start.1 = (bf16[512,256]{1,0:T(8,128)(2,1)S(1)}, bf16[512,256]{1,0:T(8,128)(2,1)S(1)}, u32[]{:S(2)}, u32[]{:S(2)}) collective-permute-start(bf16[512,256]{1,0:T(8,128)(2,1)S(1)} %reduce_sum.12), channel_id=1, source_target_pairs={{0,0},{1,1},{2,128},{3,129},{4,256},{5,257},{6,384},{7,385},{8,8},... | collective-permute-start | bytes 786440 | tf_op jit(solution)/shard_map/ppermute | solution.py:133
Sparse Core Ops, SparseCore 0:
  9.5 43.2 all-gather.6

commit v2 on v1

v2 whole, which is shorter than its diff:
```python
import functools
import math

import jax
import jax.numpy as jnp
from jax import lax
from jax.experimental import pallas as pl
from jax.experimental.pallas import tpu as pltpu
from jax.sharding import PartitionSpec as P

HD = 128
GROUP = 8
TOK = 64
NY, NZ, NX, NC = 4, 16, 4, 2
CHUNK = 4 * TOK
CHUNKS = 10
PLANE = NZ * TOK
SEG_ROWS = 16
BAND = 2 * PLANE + SEG_ROWS
MASKED = -1e30
VMEM = pl.BlockSpec(memory_space=pltpu.VMEM)

Y_GROUPS = [[y * NZ + z for y in range(NY)] for z in range(NZ)]
Z_GROUPS = [[y * NZ + z for z in range(NZ)] for y in range(NY)]
CORE_SWAP = [(t, t ^ 1) for t in range(NX * NC)]


def flat(y, z, x, c):
    return ((y * NZ + z) * NX + x) * NC + c


PLANE_GROUPS = [
    [flat(y, z, x, c) for y in range(NY) for x in range(NX)] for z in range(NZ) for c in range(NC)
]
QUERY_MOVE = [(y * NZ + z, (y - z) % NY * NZ + z) for y in range(NY) for z in range(NZ)]


def y_flip(d):
    return [(y * NZ + z, (y ^ d) * NZ + z) for y in range(NY) for z in range(NZ)]


def attend(q_ref, kv_ref, ids_ref, out_ref, score_ref):
    at_y, at_z = lax.axis_index("seq") // NZ, lax.axis_index("seq") % NZ
    rank = (at_y + at_z) % NY * NZ + at_z
    first_chunk = jnp.maximum(rank // 4 - (CHUNKS - 1), 0)
    pairs = ids_ref[...]
    ids = pairs[:, :TOK] + 128.0 * pairs[:, TOK:]
    own = ids_ref[pl.ds(rank, 1), :]
    own = own[:, :TOK] + 128.0 * own[:, TOK:]
    rows = lax.broadcasted_iota(jnp.int32, (TOK, TOK), 0)
    cols = lax.broadcasted_iota(jnp.int32, (TOK, TOK), 1)
    across = jnp.broadcast_to(own, (TOK, TOK))
    down = jnp.sum(jnp.where(rows == cols, across, 0.0), axis=1, keepdims=True)
    below = jnp.sum((across < down).astype(jnp.float32), axis=1, keepdims=True)
    head_id = jnp.min(own, axis=1, keepdims=True)
    earlier = jnp.sum(((ids == head_id) & (rows < rank)).astype(jnp.float32))
    begin = (rank * TOK).astype(jnp.float32) + jnp.where(down == head_id, -earlier, below)
    begin = begin.astype(jnp.int32)
    position = rank * TOK + lax.broadcasted_iota(jnp.int32, (TOK, 1), 0)

    queries = jnp.concatenate([q_ref[:, g * HD : (g + 1) * HD] for g in range(GROUP)], axis=0)
    best = jnp.full((GROUP * TOK, HD), MASKED, jnp.float32)

    def rows_at(i, offset):
        chunk = first_chunk + i
        return pl.ds(pl.multiple_of(chunk // 4 * BAND + chunk % 4 * CHUNK + offset, 16), CHUNK)

    for i in range(CHUNKS):
        scores = lax.dot_general(
            queries,
            kv_ref[rows_at(i, 0), :],
            (((1,), (1,)), ((), ())),
            preferred_element_type=jnp.float32,
        )
        at = (first_chunk + i) * CHUNK + lax.broadcasted_iota(jnp.int32, (TOK, CHUNK), 1)
        keep = (at >= begin) & (at <= position)
        scores = jnp.where(keep[None], scores.reshape(GROUP, TOK, CHUNK), MASKED)
        scores = scores.reshape(GROUP * TOK, CHUNK)
        score_ref[i] = scores
        best = jnp.maximum(best, jnp.maximum(scores[:, :HD], scores[:, HD:]))
    scale = math.log2(math.e) / math.sqrt(HD)
    top = jnp.max(best, axis=1, keepdims=True) * scale
    total = jnp.zeros((GROUP * TOK, HD), jnp.float32)
    mixed = jnp.zeros((GROUP * TOK, HD), jnp.float32)
    for i in range(CHUNKS):
        weights = jnp.exp2(score_ref[i] * scale - top)
        total += weights[:, :HD] + weights[:, HD:]
        mixed += jnp.dot(
            weights.astype(jnp.bfloat16),
            kv_ref[rows_at(i, PLANE), :],
            preferred_element_type=jnp.float32,
        )
    result = (mixed / jnp.sum(total, axis=1, keepdims=True)).astype(jnp.bfloat16)
    for g in range(GROUP):
        out_ref[:, g * HD : (g + 1) * HD] = result[g * TOK : (g + 1) * TOK]


def project(own, rows_ref, weight_ref, *refs):
    out_ref, picked_ref = refs[-2:]
    at_y, core = lax.axis_index("seq") // NZ, lax.axis_index("tp") % NC
    half = core if own else 1 - core
    for x in range(NX):
        for j in range(2):
            block = (2 * half + j) * 4 + (x + NY - at_y) % NY
            source = pl.ds(pl.multiple_of(block * TOK, TOK), TOK)
            picked_ref[pl.ds((2 * x + j) * TOK, TOK), :] = rows_ref[source, :]
    for d in range(NY):
        part = jnp.dot(picked_ref[...], weight_ref[d], preferred_element_type=jnp.float32)
        width = part.shape[-1]
        part = part.reshape(NX, 2, TOK, width)
        spot = pl.ds(d * NX, NX)
        for j in range(2):
            across = slice(j * width, (j + 1) * width)
            half_part = part[:, j]
            if own:
                half_part += refs[0][spot, :, across].astype(jnp.float32)
            out_ref[spot, :, across] = half_part.astype(jnp.bfloat16)


def combine(parts_ref, out_ref):
    at_x = lax.axis_index("tp") // NC
    width = out_ref.shape[1]
    for y in range(NY):
        total = parts_ref[y * NX].astype(jnp.float32)
        for x in range(1, NX):
            total += parts_ref[y * NX + x].astype(jnp.float32)
        total = total.astype(jnp.bfloat16)
        for j in range(2):
            block = 4 * j + (at_x + NY - y) % NY
            spot = pl.ds(pl.multiple_of(block * TOK, TOK), TOK)
            out_ref[spot, :] = total[:, j * width : (j + 1) * width]


def body(queries, keys, values, segment_ids, out_weight):
    width = out_weight.shape[1]
    copies = jnp.broadcast_to(out_weight[None], (NY,) + out_weight.shape)
    weights = lax.all_to_all(copies, "seq", 0, 0, axis_index_groups=Y_GROUPS, tiled=True)
    queries = lax.ppermute(queries, "seq", QUERY_MOVE)

    tag = jnp.concatenate([segment_ids % 128, segment_ids // 128])[None]
    tag = jnp.pad(tag, ((0, SEG_ROWS - 1), (0, 0))).astype(jnp.bfloat16)
    message = jnp.concatenate([keys, values, tag], axis=0)
    plane = lax.all_gather(message, "seq", axis_index_groups=Z_GROUPS)
    plane = jnp.concatenate(
        [
            plane[:, :TOK].reshape(PLANE, HD),
            plane[:, TOK : 2 * TOK].reshape(PLANE, HD),
            plane[:, 2 * TOK],
        ],
        axis=0,
    )
    bands = lax.all_gather(
        plane.astype(jnp.float16), "seq", axis_index_groups=Y_GROUPS, tiled=True
    )
    ids = bands.reshape(NY, BAND, HD)[:, 2 * PLANE :].reshape(NY * NZ, HD).astype(jnp.float32)
    bands = bands.astype(jnp.bfloat16)

    attended = pl.pallas_call(
        attend,
        out_shape=jax.ShapeDtypeStruct((TOK, GROUP * HD), jnp.bfloat16),
        in_specs=[VMEM] * 3,
        out_specs=VMEM,
        scratch_shapes=[pltpu.VMEM((CHUNKS, GROUP * TOK, CHUNK), jnp.float32)],
        compiler_params=pltpu.CompilerParams(vmem_limit_bytes=24 * 1024 * 1024),
        cost_estimate=pl.CostEstimate(
            flops=4 * GROUP * TOK * CHUNKS * CHUNK * HD,
            bytes_accessed=3 * 1024 * 1024,
            transcendentals=GROUP * TOK * CHUNKS * CHUNK,
        ),
    )(queries, bands, ids)

    rows = lax.all_gather(
        attended.astype(jnp.float16), "seq", axis_index_groups=Z_GROUPS, tiled=True
    ).astype(jnp.bfloat16)

    def projected(own, *operands):
        return pl.pallas_call(
            functools.partial(project, own),
            out_shape=jax.ShapeDtypeStruct((NY * NX, TOK, 2 * width), jnp.bfloat16),
            in_specs=[VMEM] * (1 + len(operands)),
            out_specs=VMEM,
            scratch_shapes=[pltpu.VMEM((PLANE // 2, GROUP * HD), jnp.bfloat16)],
            compiler_params=pltpu.CompilerParams(vmem_limit_bytes=24 * 1024 * 1024),
            cost_estimate=pl.CostEstimate(
                flops=PLANE * GROUP * HD * NY * width,
                bytes_accessed=6 * 1024 * 1024,
                transcendentals=0,
            ),
        )(rows, *operands)

    theirs = lax.ppermute(projected(False, weights), "tp", CORE_SWAP)
    sums = projected(True, weights, theirs)
    parts = lax.all_to_all(
        sums, ("seq", "tp"), 0, 0, axis_index_groups=PLANE_GROUPS, tiled=True
    )
    return pl.pallas_call(
        combine,
        out_shape=jax.ShapeDtypeStruct((8 * TOK, width), jnp.bfloat16),
        in_specs=[VMEM],
        out_specs=VMEM,
        compiler_params=pltpu.CompilerParams(vmem_limit_bytes=16 * 1024 * 1024),
    )(parts)


def solution(mesh):
    return jax.shard_map(
        body,
        mesh=mesh,
        in_specs=(P("seq", "tp"), P("seq", "tp"), P("seq", "tp"), P("seq"), P("tp", "seq")),
        out_specs=P("tp", "seq"),
        check_vma=False,
    )
```

time: 176 us -> 147 us (0.84)
  the two profiles are of different devices: /device:TPU:24 before, /device:TPU:32 now
where the time goes in v2:
time: 147 us
  blocking collectives  120 us (82%)
  starting transfers between devices  10.6 us (7%)
  Pallas kernels  6.98 us (5%)
  local copies, waits for them, and re-layouts  4.17 us (3%)
  waiting for transfers between devices  2.63 us (2%)
  other arithmetic  2.41 us (2%)
    all_gather x1, blocking collectives, body(): lax.all_gather(attended.astype(jnp.float16), 'seq', axis_index_groups=Z_G...  41.4 us
    all_gather x1, blocking collectives, body(): plane = lax.all_gather(message, 'seq', axis_index_groups=Z_GROUPS)  36.8 us
    all_to_all x1, blocking collectives, body(): lax.all_to_all(sums, ('seq', 'tp'), 0, 0, axis_index_groups=PLANE_GROUPS,...  22.9 us
    all_gather x1, blocking collectives, body(): lax.all_gather(plane.astype(jnp.float16), 'seq', axis_index_groups=Y_GROU...  18.6 us
    ppermute x1, starting transfers between devices, body(): queries = lax.ppermute(queries, 'seq', QUERY_MOVE)  4.91 us
    all_to_all x1, starting transfers between devices, body(): lax.all_to_all(copies, 'seq', 0, 0, axis_index_groups=Y_GROUPS, tiled=True)  3.74 us
    pallas_call x1, Pallas kernels, body(): pl.pallas_call(attend, out_shape=jax.ShapeDtypeStruct((TOK, GROUP * HD),...  3.65 us
  transfers between devices with their start and end apart: 3, of which 1 were waited for; matrix products, arithmetic and copies ran while one was open for 3% of the time, Pallas kernels for 2%

profile of v2, /device:TPU:32, one launch (start us, length us, event | category | flops | bytes accessed | tf_op | source)
XLA Modules:
  0.0 146.7 jit_solution(9726132770082731393)
XLA Ops:
  0.0 4.9 %collective-permute-start = (bf16[64,1024]{1,0:T(8,128)(2,1)}, bf16[64,1024]{1,0:T(8,128)(2,1)S(1)}, u32[]{:S(2)}, u32[]{:S(2)}) collective-permute-start(bf16[64,1024]{1,0:T(8,128)(2,1)} %param.5), channel_id=1, source_target_pairs={{0,0},{8,392},{16,272},{24,152},{32,32},{40,424},{48,304},{56,184}... | collective-permute-start | bytes 393224 | tf_op jit(solution)/shard_map/ppermute | solution.py:138
  4.9 2.5 %broadcast_in_dim.11 = bf16[4,1024,256]{2,1,0:T(8,128)(2,1)} broadcast(bf16[1024,256]{1,0:T(8,128)(2,1)} %param.9), dimensions={1,2} | broadcast | bytes 2621440 | tf_op jit(solution)/shard_map/broadcast_in_dim | solution.py:136
  7.4 3.7 %all-to-all-start = ((bf16[4,1024,256]{2,1,0:T(8,128)(2,1)}), bf16[4,1024,256]{2,1,0:T(8,128)(2,1)S(1)}, u32[]{:S(2)}, u32[]{:S(2)}) async-start(bf16[4,1024,256]{2,1,0:T(8,128)(2,1)} %broadcast_in_dim.11), calls=%async_computation | async-start | bytes 4194304 | tf_op jit(solution)/shard_map/all_to_all | solution.py:137
  11.2 0.0 copy-done.3
  11.2 0.1 maximum_bitcast_fusion
  11.3 0.0 copy-done.1
  11.3 0.0 copy-done.2
  11.3 36.8 %all-gather = bf16[2304,128]{1,0:T(8,128)(2,1)S(1)} all-gather(bf16[144,128]{1,0:T(8,128)(2,1)S(1)} %fusion.1), channel_id=2, replica_groups={{0,8,16,24,32,40,48,56,64,72,80,88,96,104,112,120},{128,136,144,152,160..., dimensions={0}, use_global_device_ids=true | all-gather | bytes 626688 | tf_op jit(solution)/shard_map/all_gather | solution.py:143
  48.1 0.1 fusion.4
  48.2 0.1 maximum_convert_fusion
  48.3 18.6 %all-gather.3 = f16[8256,128]{1,0:T(8,128)(2,1)S(1)} all-gather(f16[2064,128]{1,0:T(8,128)(2,1)S(1)} %maximum_convert_fusion), channel_id=1, replica_groups={{0,128,256,384},{8,136,264,392},{16,144,272,400},{24,152,280,408},{32,1..., dimensions={0}, use_global_device_ids=true | all-gather | bytes 2641920 | tf_op jit(solution)/shard_map/all_gather | solution.py:152
  66.9 0.3 convert_element_type.19.kv_ref
  67.2 0.0 collective-permute-done.q_ref
  67.2 3.6 %shard_map.55 = bf16[64,1024]{1,0:T(8,128)(2,1)S(1)} custom-call(bf16[64,1024]{1,0:T(8,128)(2,1)S(1)} %collective-permute-done.q_ref, bf16[8256,128]{1,0:T(8,128)(2,1)S(1)} %convert_element_type.19.kv_ref, f32[64,128]{1,0:T(8,128)S(1)} %bitcast_convert_fusion.ids_ref), custom_call_target="tpu_custom_call" | custom-call | flops 671088640 | bytes 3145728 | tf_op jit(solution)/shard_map/pallas_call | solution.py:158
  70.9 41.4 %all-gather.4 = f16[1024,1024]{1,0:T(8,128)(2,1)S(1)} all-gather(f16[64,1024]{1,0:T(8,128)(2,1)S(1)} %convert_element_type.22), channel_id=1, replica_groups={{0,8,16,24,32,40,48,56,64,72,80,88,96,104,112,120},{128,136,144,152,160..., dimensions={0}, use_global_device_ids=true | all-gather | bytes 2228224 | tf_op jit(solution)/shard_map/all_gather | solution.py:172
  112.3 1.9 %convert_element_type.23.rows_ref = bf16[1024,1024]{1,0:T(8,128)(2,1)} convert(f16[1024,1024]{1,0:T(8,128)(2,1)S(1)} %all-gather.4) | non-fusion elementwise | flops 1048576 | bytes 4194304 | tf_op jit(solution)/shard_map/convert_element_type | solution.py:174
  114.2 0.0 all-to-all-done.weight_ref
  114.2 1.6 %copy-done = bf16[1024,1024]{1,0:T(8,128)(2,1)S(1)} copy-done((bf16[1024,1024]{1,0:T(8,128)(2,1)S(1)}, bf16[1024,1024]{1,0:T(8,128)(2,1)}, u32[]{:S(2)}) %copy-start) | copy-done | bytes 2097176
  115.8 1.2 shard_map.56
  117.1 1.9 %collective-permute-start.1 = (bf16[16,64,512]{2,1,0:T(8,128)(2,1)S(1)}, bf16[16,64,512]{2,1,0:T(8,128)(2,1)S(1)}, u32[]{:S(2)}, u32[]{:S(2)}) collective-permute-start(bf16[16,64,512]{2,1,0:T(8,128)(2,1)S(1)} %shard_map.56), channel_id=1, source_target_pairs={{0,1},{1,0},{2,3},{3,2},{4,5},{5,4},{6,7},{7,6},{8,9},{9,8},{10,11... | collective-permute-start | bytes 3145736 | tf_op jit(solution)/shard_map/ppermute | solution.py:191
  119.0 2.6 %collective-permute-done.1.refs_0_ = bf16[16,64,512]{2,1,0:T(8,128)(2,1)S(1)} collective-permute-done((bf16[16,64,512]{2,1,0:T(8,128)(2,1)S(1)}, bf16[16,64,512]{2,1,0:T(8,128)(2,1)S(1)}, u32[]{:S(2)}, u32[]{:S(2)}) %collective-permute-start.1) | collective-permute-done | bytes 1048608 | tf_op jit(solution)/shard_map/ppermute | solution.py:191
  121.6 1.2 shard_map.57
  122.9 22.9 %all_to_all.10.parts_ref = bf16[16,64,512]{2,1,0:T(8,128)(2,1)S(1)} all-to-all(bf16[16,64,512]{2,1,0:T(8,128)(2,1)S(1)} %shard_map.57), channel_id=1, replica_groups={{0,2,4,6,128,130,132,134,256,258,260,262,384,386,388,390},{1,3,5,7,129,..., dimensions={0} | all-to-all | bytes 2097152 | tf_op jit(solution)/shard_map/all_to_all | solution.py:193
  145.8 0.8 shard_map.58
  (11 shorter events, 0.1 us)
Async XLA Ops:
  0.0 67.2 %collective-permute-start = (bf16[64,1024]{1,0:T(8,128)(2,1)}, bf16[64,1024]{1,0:T(8,128)(2,1)S(1)}, u32[]{:S(2)}, u32[]{:S(2)}) collective-permute-start(bf16[64,1024]{1,0:T(8,128)(2,1)} %param.5), channel_id=1, source_target_pairs={{0,0},{8,392},{16,272},{24,152},{32,32},{40,424},{48,304},{56,184}... | collective-permute-start | bytes 393224 | tf_op jit(solution)/shard_map/ppermute | solution.py:138
  7.4 3.8 %copy-start.3 = (s32[64]{0:T(128)S(1)}, s32[64]{0:T(128)}, u32[]{:S(2)}) copy-start(s32[64]{0:T(128)} %param.8) | copy-start | bytes 772
  7.4 3.9 %copy-start.1 = (bf16[64,128]{1,0:T(8,128)(2,1)S(1)}, bf16[64,128]{1,0:T(8,128)(2,1)}, u32[]{:S(2)}) copy-start(bf16[64,128]{1,0:T(8,128)(2,1)} %param.7) | copy-start | bytes 49156
  7.4 3.9 %copy-start.2 = (bf16[64,128]{1,0:T(8,128)(2,1)S(1)}, bf16[64,128]{1,0:T(8,128)(2,1)}, u32[]{:S(2)}) copy-start(bf16[64,128]{1,0:T(8,128)(2,1)} %param.6) | copy-start | bytes 49156
  7.4 106.8 %all-to-all-start = ((bf16[4,1024,256]{2,1,0:T(8,128)(2,1)}), bf16[4,1024,256]{2,1,0:T(8,128)(2,1)S(1)}, u32[]{:S(2)}, u32[]{:S(2)}) async-start(bf16[4,1024,256]{2,1,0:T(8,128)(2,1)} %broadcast_in_dim.11), calls=%async_computation | async-start | bytes 4194304 | tf_op jit(solution)/shard_map/all_to_all | solution.py:137
  114.2 1.6 %copy-start = (bf16[1024,1024]{1,0:T(8,128)(2,1)S(1)}, bf16[1024,1024]{1,0:T(8,128)(2,1)}, u32[]{:S(2)}) copy-start(bf16[1024,1024]{1,0:T(8,128)(2,1)} %convert_element_type.23.rows_ref) | copy-start | bytes 6291460
  117.1 4.6 %collective-permute-start.1 = (bf16[16,64,512]{2,1,0:T(8,128)(2,1)S(1)}, bf16[16,64,512]{2,1,0:T(8,128)(2,1)S(1)}, u32[]{:S(2)}, u32[]{:S(2)}) collective-permute-start(bf16[16,64,512]{2,1,0:T(8,128)(2,1)S(1)} %shard_map.56), channel_id=1, source_target_pairs={{0,1},{1,0},{2,3},{3,2},{4,5},{5,4},{6,7},{7,6},{8,9},{9,8},{10,11... | collective-permute-start | bytes 3145736 | tf_op jit(solution)/shard_map/ppermute | solution.py:191

commit v3 on v2

--- a/solution.py
+++ b/solution.py
@@ -13,7 +13,7 @@
 TOK = 64
 NY, NZ, NX, NC = 4, 16, 4, 2
 CHUNK = 4 * TOK
-CHUNKS = 10
+CHUNKS = 9
 PLANE = NZ * TOK
 SEG_ROWS = 16
 BAND = 2 * PLANE + SEG_ROWS
@@ -42,7 +42,7 @@
 def attend(q_ref, kv_ref, ids_ref, out_ref, score_ref):
     at_y, at_z = lax.axis_index("seq") // NZ, lax.axis_index("seq") % NZ
     rank = (at_y + at_z) % NY * NZ + at_z
-    first_chunk = jnp.maximum(rank // 4 - (CHUNKS - 1), 0)
+    first_pair = jnp.maximum(rank // 2 - (2 * CHUNKS - 1), 0)
     pairs = ids_ref[...]
     ids = pairs[:, :TOK] + 128.0 * pairs[:, TOK:]
     own = ids_ref[pl.ds(rank, 1), :]
@@ -62,17 +62,20 @@
     best = jnp.full((GROUP * TOK, HD), MASKED, jnp.float32)
 
     def rows_at(i, offset):
-        chunk = first_chunk + i
-        return pl.ds(pl.multiple_of(chunk // 4 * BAND + chunk % 4 * CHUNK + offset, 16), CHUNK)
+        parts = []
+        for pair in (first_pair + 2 * i, first_pair + 2 * i + 1):
+            start = pair // 8 * BAND + pair % 8 * (2 * TOK) + offset
+            parts.append(kv_ref[pl.ds(pl.multiple_of(start, 16), 2 * TOK), :])
+        return jnp.concatenate(parts, axis=0)
 
     for i in range(CHUNKS):
         scores = lax.dot_general(
             queries,
-            kv_ref[rows_at(i, 0), :],
+            rows_at(i, 0),
             (((1,), (1,)), ((), ())),
             preferred_element_type=jnp.float32,
         )
-        at = (first_chunk + i) * CHUNK + lax.broadcasted_iota(jnp.int32, (TOK, CHUNK), 1)
+        at = first_pair * (2 * TOK) + i * CHUNK + lax.broadcasted_iota(jnp.int32, (TOK, CHUNK), 1)
         keep = (at >= begin) & (at <= position)
         scores = jnp.where(keep[None], scores.reshape(GROUP, TOK, CHUNK), MASKED)
         scores = scores.reshape(GROUP * TOK, CHUNK)
@@ -87,7 +90,7 @@
         total += weights[:, :HD] + weights[:, HD:]
         mixed += jnp.dot(
             weights.astype(jnp.bfloat16),
-            kv_ref[rows_at(i, PLANE), :],
+            rows_at(i, PLANE),
             preferred_element_type=jnp.float32,
         )
     result = (mixed / jnp.sum(total, axis=1, keepdims=True)).astype(jnp.bfloat16)
@@ -161,7 +164,7 @@
         in_specs=[VMEM] * 3,
         out_specs=VMEM,
         scratch_shapes=[pltpu.VMEM((CHUNKS, GROUP * TOK, CHUNK), jnp.float32)],
-        compiler_params=pltpu.CompilerParams(vmem_limit_bytes=24 * 1024 * 1024),
+        compiler_params=pltpu.CompilerParams(vmem_limit_bytes=16 * 1024 * 1024),
         cost_estimate=pl.CostEstimate(
             flops=4 * GROUP * TOK * CHUNKS * CHUNK * HD,
             bytes_accessed=3 * 1024 * 1024,
@@ -169,6 +172,7 @@
         ),
     )(queries, bands, ids)
 
+    attended, weights = lax.optimization_barrier((attended, weights))
     rows = lax.all_gather(
         attended.astype(jnp.float16), "seq", axis_index_groups=Z_GROUPS, tiled=True
     ).astype(jnp.bfloat16)
@@ -180,7 +184,7 @@
             in_specs=[VMEM] * (1 + len(operands)),
             out_specs=VMEM,
             scratch_shapes=[pltpu.VMEM((PLANE // 2, GROUP * HD), jnp.bfloat16)],
-            compiler_params=pltpu.CompilerParams(vmem_limit_bytes=24 * 1024 * 1024),
+            compiler_params=pltpu.CompilerParams(vmem_limit_bytes=16 * 1024 * 1024),
             cost_estimate=pl.CostEstimate(
                 flops=PLANE * GROUP * HD * NY * width,
                 bytes_accessed=6 * 1024 * 1024,

time: 147 us -> 144 us (0.980)
  local copies, waits for them, and re-layouts: 4.17 us -> 2.6 us
    unnamed x9 -> x7, local copies, waits for them, and re-layouts: 1.61 us -> 0.01 us
  transfers between devices with their start and end apart: 3 -> 3, of which waited for: 1 -> 1; matrix products, arithmetic and copies ran while one was open for 3% -> 2% of each run, Pallas kernels for 2% -> 2%
where the time goes in v3:
time: 144 us; the launch traced here: 143 us
  blocking collectives  120 us (83%)
  starting transfers between devices  10.6 us (7%)
  Pallas kernels  6.69 us (5%)
  waiting for transfers between devices  2.63 us (2%)
  local copies, waits for them, and re-layouts  2.6 us (2%)
    all_gather x1, blocking collectives, body(): lax.all_gather(attended.astype(jnp.float16), 'seq', axis_index_groups=Z_G...  41.4 us
    all_gather x1, blocking collectives, body(): plane = lax.all_gather(message, 'seq', axis_index_groups=Z_GROUPS)  36.8 us
    all_to_all x1, blocking collectives, body(): lax.all_to_all(sums, ('seq', 'tp'), 0, 0, axis_index_groups=PLANE_GROUPS,...  22.9 us
    all_gather x1, blocking collectives, body(): lax.all_gather(plane.astype(jnp.float16), 'seq', axis_index_groups=Y_GROU...  18.6 us
    ppermute x1, starting transfers between devices, body(): queries = lax.ppermute(queries, 'seq', QUERY_MOVE)  4.91 us
    all_to_all x1, starting transfers between devices, body(): lax.all_to_all(copies, 'seq', 0, 0, axis_index_groups=Y_GROUPS, tiled=True)  3.74 us
    pallas_call x1, Pallas kernels, body(): pl.pallas_call(attend, out_shape=jax.ShapeDtypeStruct((TOK, GROUP * HD),...  3.34 us
  transfers between devices with their start and end apart: 3, of which 1 were waited for; matrix products, arithmetic and copies ran while one was open for 2% of the time, Pallas kernels for 2%

profile of v3, /device:TPU:32, one launch (start us, length us, event | category | flops | bytes accessed | tf_op | source)
XLA Modules:
  0.0 143.5 jit_solution(14031828214333226455)
XLA Ops:
  0.0 4.9 %collective-permute-start = (bf16[64,1024]{1,0:T(8,128)(2,1)}, bf16[64,1024]{1,0:T(8,128)(2,1)S(1)}, u32[]{:S(2)}, u32[]{:S(2)}) collective-permute-start(bf16[64,1024]{1,0:T(8,128)(2,1)} %param.5), channel_id=1, source_target_pairs={{0,0},{8,392},{16,272},{24,152},{32,32},{40,424},{48,304},{56,184}... | collective-permute-start | bytes 393224 | tf_op jit(solution)/shard_map/ppermute | solution.py:141
  4.9 2.5 %broadcast_in_dim.11 = bf16[4,1024,256]{2,1,0:T(8,128)(2,1)} broadcast(bf16[1024,256]{1,0:T(8,128)(2,1)} %param.9), dimensions={1,2} | broadcast | bytes 2621440 | tf_op jit(solution)/shard_map/broadcast_in_dim | solution.py:139
  7.4 0.0 copy-start.2
  7.4 3.7 %all-to-all-start = ((bf16[4,1024,256]{2,1,0:T(8,128)(2,1)}), bf16[4,1024,256]{2,1,0:T(8,128)(2,1)S(1)}, u32[]{:S(2)}, u32[]{:S(2)}) async-start(bf16[4,1024,256]{2,1,0:T(8,128)(2,1)} %broadcast_in_dim.11), calls=%async_computation | async-start | bytes 4194304 | tf_op jit(solution)/shard_map/all_to_all | solution.py:140
  11.2 0.0 copy-done.2
  11.2 0.1 maximum_bitcast_fusion
  11.3 0.0 copy-done
  11.3 0.0 copy-done.1
  11.3 36.8 %all-gather = bf16[2304,128]{1,0:T(8,128)(2,1)S(1)} all-gather(bf16[144,128]{1,0:T(8,128)(2,1)S(1)} %fusion.1), channel_id=2, replica_groups={{0,8,16,24,32,40,48,56,64,72,80,88,96,104,112,120},{128,136,144,152,160..., dimensions={0}, use_global_device_ids=true | all-gather | bytes 626688 | tf_op jit(solution)/shard_map/all_gather | solution.py:146
  48.2 0.1 fusion.4
  48.2 0.1 maximum_convert_fusion
  48.3 18.6 %all-gather.3 = f16[8256,128]{1,0:T(8,128)(2,1)S(1)} all-gather(f16[2064,128]{1,0:T(8,128)(2,1)S(1)} %maximum_convert_fusion), channel_id=1, replica_groups={{0,128,256,384},{8,136,264,392},{16,144,272,400},{24,152,280,408},{32,1..., dimensions={0}, use_global_device_ids=true | all-gather | bytes 2641920 | tf_op jit(solution)/shard_map/all_gather | solution.py:155
  66.9 0.3 convert_element_type.19.kv_ref
  67.2 0.0 collective-permute-done.q_ref
  67.2 3.3 %shard_map.55 = bf16[64,1024]{1,0:T(8,128)(2,1)S(1)} custom-call(bf16[64,1024]{1,0:T(8,128)(2,1)S(1)} %collective-permute-done.q_ref, bf16[8256,128]{1,0:T(8,128)(2,1)S(1)} %convert_element_type.19.kv_ref, f32[64,128]{1,0:T(8,128)S(1)} %bitcast_convert_fusion.ids_ref), custom_call_target="tpu_custom_call" | custom-call | flops 603979776 | bytes 3145728 | tf_op jit(solution)/shard_map/pallas_call | solution.py:161
  70.6 0.0 all-to-all-done.weight_ref
  70.6 41.4 %all-gather.4 = f16[1024,1024]{1,0:T(8,128)(2,1)S(1)} all-gather(f16[64,1024]{1,0:T(8,128)(2,1)S(1)} %convert_element_type.22), channel_id=1, replica_groups={{0,8,16,24,32,40,48,56,64,72,80,88,96,104,112,120},{128,136,144,152,160..., dimensions={0}, use_global_device_ids=true | all-gather | bytes 2228224 | tf_op jit(solution)/shard_map/all_gather | solution.py:176
  112.0 0.6 convert_element_type.23.rows_ref
  112.6 1.3 shard_map.56
  113.9 1.9 %collective-permute-start.1 = (bf16[16,64,512]{2,1,0:T(8,128)(2,1)S(1)}, bf16[16,64,512]{2,1,0:T(8,128)(2,1)S(1)}, u32[]{:S(2)}, u32[]{:S(2)}) collective-permute-start(bf16[16,64,512]{2,1,0:T(8,128)(2,1)S(1)} %shard_map.56), channel_id=1, source_target_pairs={{0,1},{1,0},{2,3},{3,2},{4,5},{5,4},{6,7},{7,6},{8,9},{9,8},{10,11... | collective-permute-start | bytes 3145736 | tf_op jit(solution)/shard_map/ppermute | solution.py:195
  115.8 2.6 %collective-permute-done.1.refs_0_ = bf16[16,64,512]{2,1,0:T(8,128)(2,1)S(1)} collective-permute-done((bf16[16,64,512]{2,1,0:T(8,128)(2,1)S(1)}, bf16[16,64,512]{2,1,0:T(8,128)(2,1)S(1)}, u32[]{:S(2)}, u32[]{:S(2)}) %collective-permute-start.1) | collective-permute-done | bytes 1048608 | tf_op jit(solution)/shard_map/ppermute | solution.py:195
  118.4 1.3 shard_map.57
  119.7 22.9 %all_to_all.10.parts_ref = bf16[16,64,512]{2,1,0:T(8,128)(2,1)S(1)} all-to-all(bf16[16,64,512]{2,1,0:T(8,128)(2,1)S(1)} %shard_map.57), channel_id=1, replica_groups={{0,2,4,6,128,130,132,134,256,258,260,262,384,386,388,390},{1,3,5,7,129,..., dimensions={0} | all-to-all | bytes 2097152 | tf_op jit(solution)/shard_map/all_to_all | solution.py:197
  142.7 0.8 shard_map.58
  (9 shorter events, 0.1 us)
Async XLA Ops:
  0.0 67.2 %collective-permute-start = (bf16[64,1024]{1,0:T(8,128)(2,1)}, bf16[64,1024]{1,0:T(8,128)(2,1)S(1)}, u32[]{:S(2)}, u32[]{:S(2)}) collective-permute-start(bf16[64,1024]{1,0:T(8,128)(2,1)} %param.5), channel_id=1, source_target_pairs={{0,0},{8,392},{16,272},{24,152},{32,32},{40,424},{48,304},{56,184}... | collective-permute-start | bytes 393224 | tf_op jit(solution)/shard_map/ppermute | solution.py:141
  7.4 3.8 %copy-start.2 = (s32[64]{0:T(128)S(1)}, s32[64]{0:T(128)}, u32[]{:S(2)}) copy-start(s32[64]{0:T(128)} %param.8) | copy-start | bytes 772
  7.4 3.9 %copy-start = (bf16[64,128]{1,0:T(8,128)(2,1)S(1)}, bf16[64,128]{1,0:T(8,128)(2,1)}, u32[]{:S(2)}) copy-start(bf16[64,128]{1,0:T(8,128)(2,1)} %param.7) | copy-start | bytes 49156
  7.4 3.9 %copy-start.1 = (bf16[64,128]{1,0:T(8,128)(2,1)S(1)}, bf16[64,128]{1,0:T(8,128)(2,1)}, u32[]{:S(2)}) copy-start(bf16[64,128]{1,0:T(8,128)(2,1)} %param.6) | copy-start | bytes 49156
  7.4 63.1 %all-to-all-start = ((bf16[4,1024,256]{2,1,0:T(8,128)(2,1)}), bf16[4,1024,256]{2,1,0:T(8,128)(2,1)S(1)}, u32[]{:S(2)}, u32[]{:S(2)}) async-start(bf16[4,1024,256]{2,1,0:T(8,128)(2,1)} %broadcast_in_dim.11), calls=%async_computation | async-start | bytes 4194304 | tf_op jit(solution)/shard_map/all_to_all | solution.py:140
  113.9 4.6 %collective-permute-start.1 = (bf16[16,64,512]{2,1,0:T(8,128)(2,1)S(1)}, bf16[16,64,512]{2,1,0:T(8,128)(2,1)S(1)}, u32[]{:S(2)}, u32[]{:S(2)}) collective-permute-start(bf16[16,64,512]{2,1,0:T(8,128)(2,1)S(1)} %shard_map.56), channel_id=1, source_target_pairs={{0,1},{1,0},{2,3},{3,2},{4,5},{5,4},{6,7},{7,6},{8,9},{9,8},{10,11... | collective-permute-start | bytes 3145736 | tf_op jit(solution)/shard_map/ppermute | solution.py:195

commit v4 on v3

v4 whole, which is shorter than its diff:
```python
import functools
import math

import jax
import jax.numpy as jnp
from jax import lax
from jax.experimental import pallas as pl
from jax.experimental.pallas import tpu as pltpu
from jax.sharding import PartitionSpec as P

HD = 128
GROUP = 8
TOK = 64
NY, NZ, NX, NC = 4, 16, 4, 2
CHUNK = 4 * TOK
CHUNKS = NZ // 4
HEADS_AT_ONCE = 4
PLANE = NZ * TOK
SEG_ROWS = 16
WEIGHT_ROWS = GROUP * HD
QUERY_ROWS = GROUP * TOK // 2
SENT_ROWS = WEIGHT_ROWS + QUERY_ROWS + SEG_ROWS
WIDE = GROUP * HD + 128
MASKED = -1e30
VMEM = pl.BlockSpec(memory_space=pltpu.VMEM)
ANY = pl.BlockSpec(memory_space=pl.ANY)

Y_GROUPS = [[y * NZ + z for y in range(NY)] for z in range(NZ)]
Z_GROUPS = [[y * NZ + z for z in range(NZ)] for y in range(NY)]
CORE_SWAP = [(t, t ^ 1) for t in range(NX * NC)]


def flat(y, z, x, c):
    return ((y * NZ + z) * NX + x) * NC + c


PLANE_GROUPS = [
    [flat(y, z, x, c) for y in range(NY) for x in range(NX)] for z in range(NZ) for c in range(NC)
]
def attend(sent_ref, plane_ref, out_ref, score_ref):
    at_y, at_z = lax.axis_index("seq") // NZ, lax.axis_index("seq") % NZ
    scale = math.log2(math.e) / math.sqrt(HD)
    count = HEADS_AT_ONCE * TOK
    rows = lax.broadcasted_iota(jnp.int32, (TOK, TOK), 0)
    cols = lax.broadcasted_iota(jnp.int32, (TOK, TOK), 1)
    lane = lax.broadcasted_iota(jnp.int32, (TOK, 128), 1)
    position = at_z * TOK + lax.broadcasted_iota(jnp.int32, (TOK, 1), 0)

    def ids_of(tile):
        pair = tile.astype(jnp.float32)[:1, : 2 * TOK]
        return pair[:, :TOK] + 128.0 * pair[:, TOK:]

    def part_of(i, start):
        return jnp.concatenate(
            [plane_ref[4 * i + j, start : start + TOK] for j in range(4)], axis=0
        )

    def key_ids(i):
        return jnp.concatenate(
            [ids_of(plane_ref[4 * i + j, 2 * TOK :]) for j in range(4)], axis=1
        )

    def band(ahead, chunks):
        y = at_y + ahead
        slot = (y + NY - at_z % NY) % NY
        own = ids_of(sent_ref[y, WEIGHT_ROWS + QUERY_ROWS :, :])
        own = jnp.sum(jnp.where(rows == cols, own, 0.0), axis=1, keepdims=True)
        keys = [part_of(i, 0) for i in chunks]
        values = [part_of(i, TOK) for i in chunks]
        keeps = []
        for i in chunks:
            keep = key_ids(i) == own
            if ahead == 0:
                at = i * CHUNK + lax.broadcasted_iota(jnp.int32, (TOK, CHUNK), 1)
                keep = keep & (at <= position)
            keeps.append(keep)
        marks = jnp.zeros((TOK, 128), jnp.float32)
        for first in range(0, GROUP, HEADS_AT_ONCE):
            heads = range(first, first + HEADS_AT_ONCE)
            queries = []
            for g in heads:
                row = WEIGHT_ROWS + g // 2 * TOK
                queries.append(sent_ref[y, row : row + TOK, g % 2 * HD : (g % 2 + 1) * HD])
            queries = jnp.concatenate(queries, axis=0)
            held = slice(first * TOK, first * TOK + count)
            best = jnp.full((count, HD), MASKED, jnp.float32)
            for n in range(len(chunks)):
                scores = lax.dot_general(
                    queries, keys[n], (((1,), (1,)), ((), ())), preferred_element_type=jnp.float32
                )
                scores = scores.reshape(HEADS_AT_ONCE, TOK, CHUNK)
                scores = jnp.where(keeps[n][None], scores, MASKED).reshape(count, CHUNK)
                score_ref[n, held] = scores
                best = jnp.maximum(best, jnp.maximum(scores[:, :HD], scores[:, HD:]))
            top = jnp.max(best, axis=1, keepdims=True) * scale
            total = jnp.zeros((count, HD), jnp.float32)
            mixed = jnp.zeros((count, HD), jnp.float32)
            for n in range(len(chunks)):
                weights = jnp.exp2(score_ref[n, held] * scale - top)
                total += weights[:, :HD] + weights[:, HD:]
                mixed += jnp.dot(
                    weights.astype(jnp.bfloat16), values[n], preferred_element_type=jnp.float32
                )
            total = jnp.sum(total, axis=1, keepdims=True)
            result = (mixed / total).astype(jnp.bfloat16)
            level = top + jnp.log2(total)
            high = level.astype(jnp.bfloat16).astype(jnp.float32)
            middle = (level - high).astype(jnp.bfloat16).astype(jnp.float32)
            for place, g in enumerate(heads):
                here = slice(place * TOK, (place + 1) * TOK)
                out_ref[slot, :, g * HD : (g + 1) * HD] = result[here]
                marks = jnp.where(lane == g, high[here], marks)
                marks = jnp.where(lane == GROUP + g, middle[here], marks)
                rest = level[here] - high[here] - middle[here]
                marks = jnp.where(lane == 2 * GROUP + g, rest, marks)
        out_ref[slot, :, GROUP * HD :] = marks.astype(jnp.bfloat16)

    for ahead in range(NY):
        seen = at_y + ahead < NY
        if ahead == 3:
            seen = seen & (at_z == 0)

        @pl.when(seen)
        def _(ahead=ahead):
            band(ahead, list(range(CHUNKS)) if ahead < 3 else [CHUNKS - 1])

        @pl.when(jnp.logical_not(seen))
        def _(ahead=ahead):
            slot = (at_y + ahead + NY - at_z % NY) % NY
            out_ref[slot, :, : GROUP * HD] = jnp.zeros((TOK, GROUP * HD), jnp.bfloat16)
            marks = jnp.where(lane < GROUP, MASKED, 0.0)
            out_ref[slot, :, GROUP * HD :] = marks.astype(jnp.bfloat16)


def merge(parts_ref, out_ref):
    levels = []
    for y in range(NY):
        marks = parts_ref[y, :, GROUP * HD :].astype(jnp.float32)
        levels.append(
            marks[:, :GROUP] + marks[:, GROUP : 2 * GROUP] + marks[:, 2 * GROUP : 3 * GROUP]
        )
    top = functools.reduce(jnp.maximum, levels)
    shares = [jnp.exp2(level - top) for level in levels]
    whole = sum(shares)
    shares = [share / whole for share in shares]
    for g in range(GROUP):
        across = slice(g * HD, (g + 1) * HD)
        total = jnp.zeros((TOK, HD), jnp.float32)
        for y in range(NY):
            total += shares[y][:, g : g + 1] * parts_ref[y, :, across].astype(jnp.float32)
        out_ref[:, across] = total.astype(jnp.bfloat16)


def project(own, rows_ref, weight_ref, *refs):
    out_ref, picked_ref = refs[-2:]
    at_y, core = lax.axis_index("seq") // NZ, lax.axis_index("tp") % NC
    half = core if own else 1 - core
    for x in range(NX):
        for j in range(2):
            block = (2 * half + j) * 4 + (x + NY - at_y) % NY
            source = pl.ds(pl.multiple_of(block * TOK, TOK), TOK)
            picked_ref[pl.ds((2 * x + j) * TOK, TOK), :] = rows_ref[source, :]
    for d in range(NY):
        part = jnp.dot(picked_ref[...], weight_ref[d, :WEIGHT_ROWS], preferred_element_type=jnp.float32)
        width = part.shape[-1]
        part = part.reshape(NX, 2, TOK, width)
        spot = pl.ds(d * NX, NX)
        for j in range(2):
            across = slice(j * width, (j + 1) * width)
            half_part = part[:, j]
            if own:
                half_part += refs[0][spot, :, across].astype(jnp.float32)
            out_ref[spot, :, across] = half_part.astype(jnp.bfloat16)


def combine(parts_ref, out_ref):
    at_x = lax.axis_index("tp") // NC
    width = out_ref.shape[1]
    for y in range(NY):
        total = parts_ref[y * NX].astype(jnp.float32)
        for x in range(1, NX):
            total += parts_ref[y * NX + x].astype(jnp.float32)
        total = total.astype(jnp.bfloat16)
        for j in range(2):
            block = 4 * j + (at_x + NY - y) % NY
            spot = pl.ds(pl.multiple_of(block * TOK, TOK), TOK)
            out_ref[spot, :] = total[:, j * width : (j + 1) * width]


def spread(weight_ref, q_ref, ids_ref, out_ref, held_ref, own_ref, in_sems, out_sems):
    width = weight_ref.shape[1]
    half = WEIGHT_ROWS // 2
    arrivals = []
    for piece in range(2):
        part = pl.ds(piece * half, half)
        copy = pltpu.make_async_copy(weight_ref.at[part], held_ref.at[part], in_sems.at[piece])
        arrivals.append((part, [copy]))
    pieces = []
    for k in range(q_ref.shape[1] // width):
        target = held_ref.at[pl.ds(WEIGHT_ROWS + k * TOK, TOK)]
        source = q_ref.at[:, pl.ds(k * width, width)]
        pieces.append(pltpu.make_async_copy(source, target, in_sems.at[2 + k]))
    arrivals.append((pl.ds(WEIGHT_ROWS, SENT_ROWS - WEIGHT_ROWS), pieces))
    fetch = pltpu.make_async_copy(ids_ref, own_ref, in_sems.at[6])
    fetch.start()
    for _, copies in arrivals:
        for copy in copies:
            copy.start()
    leaving = []
    for index, (part, copies) in enumerate(arrivals):
        for copy in copies:
            copy.wait()
        if index == 2:
            fetch.wait()
            ids = own_ref[...]
            both = jnp.concatenate([ids & 127, ids >> 7, ids & 0, ids & 0], axis=1)
            both = jnp.broadcast_to(both.astype(jnp.float32), (SEG_ROWS, width))
            held_ref[WEIGHT_ROWS + QUERY_ROWS :] = both.astype(jnp.bfloat16)
        for y in range(NY):
            copy = pltpu.make_async_copy(
                held_ref.at[part], out_ref.at[y, part], out_sems.at[index, y]
            )
            copy.start()
            leaving.append(copy)
    for copy in leaving:
        copy.wait()


def body(queries, keys, values, segment_ids, out_weight):
    width = out_weight.shape[1]
    copies = pl.pallas_call(
        spread,
        out_shape=jax.ShapeDtypeStruct((NY, SENT_ROWS, width), jnp.bfloat16),
        in_specs=[ANY] * 3,
        out_specs=ANY,
        scratch_shapes=[
            pltpu.VMEM((SENT_ROWS, width), jnp.bfloat16),
            pltpu.VMEM((1, TOK), jnp.int32),
            pltpu.SemaphoreType.DMA((7,)),
            pltpu.SemaphoreType.DMA((3, NY)),
        ],
        compiler_params=pltpu.CompilerParams(vmem_limit_bytes=60 * 1024 * 1024),
    )(out_weight, queries, segment_ids.reshape(1, TOK))
    sent = lax.all_to_all(copies, "seq", 0, 0, axis_index_groups=Y_GROUPS, tiled=True)

    tag = jnp.concatenate([segment_ids % 128, segment_ids // 128])[None]
    tag = jnp.pad(tag, ((0, SEG_ROWS - 1), (0, 0))).astype(jnp.bfloat16)
    message = jnp.concatenate([keys, values, tag], axis=0)
    plane = lax.all_gather(message, "seq", axis_index_groups=Z_GROUPS)

    parts = pl.pallas_call(
        attend,
        out_shape=jax.ShapeDtypeStruct((NY, TOK, WIDE), jnp.bfloat16),
        in_specs=[VMEM] * 2,
        out_specs=VMEM,
        scratch_shapes=[pltpu.VMEM((CHUNKS, GROUP * TOK, CHUNK), jnp.float32)],
        compiler_params=pltpu.CompilerParams(vmem_limit_bytes=16 * 1024 * 1024),
        cost_estimate=pl.CostEstimate(
            flops=12 * GROUP * TOK * CHUNKS * CHUNK * HD,
            bytes_accessed=3 * 1024 * 1024,
            transcendentals=3 * GROUP * TOK * CHUNKS * CHUNK,
        ),
    )(sent, plane)
    parts = lax.all_to_all(parts, "seq", 0, 0, axis_index_groups=Y_GROUPS, tiled=True)
    attended = pl.pallas_call(
        merge,
        out_shape=jax.ShapeDtypeStruct((TOK, GROUP * HD), jnp.bfloat16),
        in_specs=[VMEM],
        out_specs=VMEM,
        compiler_params=pltpu.CompilerParams(vmem_limit_bytes=16 * 1024 * 1024),
    )(parts)

    rows = lax.all_gather(
        attended.astype(jnp.float16), "seq", axis_index_groups=Z_GROUPS, tiled=True
    ).astype(jnp.bfloat16)

    def projected(own, *operands):
        return pl.pallas_call(
            functools.partial(project, own),
            out_shape=jax.ShapeDtypeStruct((NY * NX, TOK, 2 * width), jnp.bfloat16),
            in_specs=[VMEM] * (1 + len(operands)),
            out_specs=VMEM,
            scratch_shapes=[pltpu.VMEM((PLANE // 2, GROUP * HD), jnp.bfloat16)],
            compiler_params=pltpu.CompilerParams(vmem_limit_bytes=16 * 1024 * 1024),
            cost_estimate=pl.CostEstimate(
                flops=PLANE * GROUP * HD * NY * width,
                bytes_accessed=6 * 1024 * 1024,
                transcendentals=0,
            ),
        )(rows, *operands)

    theirs = lax.ppermute(projected(False, sent), "tp", CORE_SWAP)
    sums = projected(True, sent, theirs)
    parts = lax.all_to_all(
        sums, ("seq", "tp"), 0, 0, axis_index_groups=PLANE_GROUPS, tiled=True
    )
    return pl.pallas_call(
        combine,
        out_shape=jax.ShapeDtypeStruct((8 * TOK, width), jnp.bfloat16),
        in_specs=[VMEM],
        out_specs=VMEM,
        compiler_params=pltpu.CompilerParams(vmem_limit_bytes=16 * 1024 * 1024),
    )(parts)


def solution(mesh):
    return jax.shard_map(
        body,
        mesh=mesh,
        in_specs=(P("seq", "tp"), P("seq", "tp"), P("seq", "tp"), P("seq"), P("tp", "seq")),
        out_specs=P("tp", "seq"),
        check_vma=False,
    )
```

time: 144 us -> 136 us (0.944)
  starting transfers between devices: 10.6 us -> 6.53 us
  blocking collectives: 120 us -> 116 us
  Pallas kernels: 6.69 us -> 10.1 us
  local copies, waits for them, and re-layouts: 2.6 us -> 0.02 us
    all_gather x1 -> x0, blocking collectives: 18.6 us -> none  [body(): lax.all_gather(plane.astype(jnp.float16), 'seq', axis_index_groups=Y_GROU...]
    all_to_all x0 -> x1, blocking collectives: none -> 12 us  [body(): lax.all_to_all(parts, 'seq', 0, 0, axis_index_groups=Y_GROUPS, tiled=True)]
    ppermute x2 -> x1, starting transfers between devices: 6.83 us -> 1.92 us  [body(): theirs = lax.ppermute(projected(False, sent), 'tp', CORE_SWAP)]
    pallas_call x1 -> x3, Pallas kernels: 3.34 us -> 6.79 us  [the longest x1 3.69 us: body(): pl.pallas_call(attend, out_shape=jax.ShapeDtypeStruct((NY, TOK, WIDE), jn...]
    all_gather x1, blocking collectives: 41.4 us -> 44.6 us  [body(): lax.all_gather(attended.astype(jnp.float16), 'seq', axis_index_groups=Z_G...]
    broadcast_in_dim x1 -> x0, local copies, waits for them, and re-layouts: 2.52 us -> none  [body(): copies = jnp.broadcast_to(out_weight[None], (NY,) + out_weight.shape)]
  transfers between devices with their start and end apart: 3 -> 2, of which waited for: 1 -> 1; matrix products, arithmetic and copies ran while one was open for 2% -> 0% of each run, Pallas kernels for 2% -> 0%
where the time goes in v4:
time: 136 us
  blocking collectives  116 us (85%)
  Pallas kernels  10.1 us (7%)
  starting transfers between devices  6.53 us (5%)
  waiting for transfers between devices  2.63 us (2%)
    all_gather x1, blocking collectives, body(): lax.all_gather(attended.astype(jnp.float16), 'seq', axis_index_groups=Z_G...  44.6 us
    all_gather x1, blocking collectives, body(): plane = lax.all_gather(message, 'seq', axis_index_groups=Z_GROUPS)  36.7 us
    all_to_all x1, blocking collectives, body(): lax.all_to_all(sums, ('seq', 'tp'), 0, 0, axis_index_groups=PLANE_GROUPS,...  22.3 us
    all_to_all x1, blocking collectives, body(): lax.all_to_all(parts, 'seq', 0, 0, axis_index_groups=Y_GROUPS, tiled=True)  12 us
    all_to_all x1, starting transfers between devices, body(): lax.all_to_all(copies, 'seq', 0, 0, axis_index_groups=Y_GROUPS, tiled=True)  4.61 us
    pallas_call x1, Pallas kernels, body(): pl.pallas_call(attend, out_shape=jax.ShapeDtypeStruct((NY, TOK, WIDE), jn...  3.69 us
  transfers between devices with their start and end apart: 2, of which 1 were waited for; matrix products, arithmetic and copies ran while one was open for 0% of the time, Pallas kernels for 0%

profile of v4, /device:TPU:32, one launch (start us, length us, event | category | flops | bytes accessed | tf_op | source)
XLA Modules:
  0.0 135.6 jit_solution(3895201932982697805)
XLA Ops:
  0.0 2.6 %shard_map.55 = bf16[4,1296,256]{2,1,0:T(8,128)(2,1)} custom-call(bf16[1024,256]{1,0:T(8,128)(2,1)} %weight_ref.1, bf16[64,1024]{1,0:T(8,128)(2,1)} %q_ref.1, s32[1,64]{1,0:T(1,128)} %bitcast.5), custom_call_target="tpu_custom_call" | custom-call | tf_op jit(solution)/shard_map/pallas_call | solution.py:231
  2.6 0.0 copy-start.2
  2.6 0.0 copy-start
  2.6 0.0 copy-start.1
  2.7 4.6 %all-to-all-start = ((bf16[4,1296,256]{2,1,0:T(8,128)(2,1)}), bf16[4,1296,256]{2,1,0:T(8,128)(2,1)S(1)}, u32[]{:S(2)}, u32[]{:S(2)}) async-start(bf16[4,1296,256]{2,1,0:T(8,128)(2,1)} %shard_map.55), calls=%async_computation | async-start | bytes 5308416 | tf_op jit(solution)/shard_map/all_to_all | solution.py:244
  7.3 0.0 copy-done.2
  7.3 0.1 maximum_bitcast_fusion
  7.4 0.0 copy-done
  7.4 0.0 copy-done.1
  7.4 36.7 %all-gather = bf16[2304,128]{1,0:T(8,128)(2,1)S(1)} all-gather(bf16[144,128]{1,0:T(8,128)(2,1)S(1)} %fusion.1), channel_id=2, replica_groups={{0,8,16,24,32,40,48,56,64,72,80,88,96,104,112,120},{128,136,144,152,160..., dimensions={0}, use_global_device_ids=true | all-gather | bytes 626688 | tf_op jit(solution)/shard_map/all_gather | solution.py:249
  44.0 0.0 all-to-all-done.sent_ref.weight_ref
  44.0 3.7 %shard_map.56 = bf16[4,64,1152]{2,1,0:T(8,128)(2,1)S(1)} custom-call(bf16[4,1296,256]{2,1,0:T(8,128)(2,1)S(1)} %all-to-all-done.sent_ref.weight_ref, bf16[16,144,128]{2,1,0:T(8,128)(2,1)S(1)} %bitcast.4), custom_call_target="tpu_custom_call" | custom-call | flops 805306368 | bytes 3145728 | tf_op jit(solution)/shard_map/pallas_call | solution.py:251
  47.8 12.0 %all_to_all.15.parts_ref = bf16[4,64,1152]{2,1,0:T(8,128)(2,1)S(1)} all-to-all(bf16[4,64,1152]{2,1,0:T(8,128)(2,1)S(1)} %shard_map.56), channel_id=1, replica_groups={{0,128,256,384},{8,136,264,392},{16,144,272,400},{24,152,280,408},{32,1..., dimensions={0} | all-to-all | bytes 1179648 | tf_op jit(solution)/shard_map/all_to_all | solution.py:264
  59.8 0.5 shard_map.57
  60.3 44.6 %all-gather.2 = f16[1024,1024]{1,0:T(8,128)(2,1)S(1)} all-gather(f16[64,1024]{1,0:T(8,128)(2,1)S(1)} %convert_element_type.7), channel_id=1, replica_groups={{0,8,16,24,32,40,48,56,64,72,80,88,96,104,112,120},{128,136,144,152,160..., dimensions={0}, use_global_device_ids=true | all-gather | bytes 2228224 | tf_op jit(solution)/shard_map/all_gather | solution.py:273
  104.9 0.6 convert_element_type.8.rows_ref
  105.4 1.3 shard_map.58
  106.7 1.9 %collective-permute-start = (bf16[16,64,512]{2,1,0:T(8,128)(2,1)S(1)}, bf16[16,64,512]{2,1,0:T(8,128)(2,1)S(1)}, u32[]{:S(2)}, u32[]{:S(2)}) collective-permute-start(bf16[16,64,512]{2,1,0:T(8,128)(2,1)S(1)} %shard_map.58), channel_id=1, source_target_pairs={{0,1},{1,0},{2,3},{3,2},{4,5},{5,4},{6,7},{7,6},{8,9},{9,8},{10,11... | collective-permute-start | bytes 3145736 | tf_op jit(solution)/shard_map/ppermute | solution.py:292
  108.6 2.6 %collective-permute-done.refs_0_ = bf16[16,64,512]{2,1,0:T(8,128)(2,1)S(1)} collective-permute-done((bf16[16,64,512]{2,1,0:T(8,128)(2,1)S(1)}, bf16[16,64,512]{2,1,0:T(8,128)(2,1)S(1)}, u32[]{:S(2)}, u32[]{:S(2)}) %collective-permute-start) | collective-permute-done | bytes 1048608 | tf_op jit(solution)/shard_map/ppermute | solution.py:292
  111.3 1.3 shard_map.59
  112.5 22.3 %all_to_all.16.parts_ref = bf16[16,64,512]{2,1,0:T(8,128)(2,1)S(1)} all-to-all(bf16[16,64,512]{2,1,0:T(8,128)(2,1)S(1)} %shard_map.59), channel_id=1, replica_groups={{0,2,4,6,128,130,132,134,256,258,260,262,384,386,388,390},{1,3,5,7,129,..., dimensions={0} | all-to-all | bytes 2097152 | tf_op jit(solution)/shard_map/all_to_all | solution.py:294
  134.8 0.8 shard_map.60
  (3 shorter events, 0.0 us)
Async XLA Ops:
  2.6 4.6 %copy-start.2 = (s32[64]{0:T(128)S(1)}, s32[64]{0:T(128)}, u32[]{:S(2)}) copy-start(s32[64]{0:T(128)} %param.8) | copy-start | bytes 772
  2.6 4.7 %copy-start = (bf16[64,128]{1,0:T(8,128)(2,1)S(1)}, bf16[64,128]{1,0:T(8,128)(2,1)}, u32[]{:S(2)}) copy-start(bf16[64,128]{1,0:T(8,128)(2,1)} %param.7) | copy-start | bytes 49156
  2.6 4.7 %copy-start.1 = (bf16[64,128]{1,0:T(8,128)(2,1)S(1)}, bf16[64,128]{1,0:T(8,128)(2,1)}, u32[]{:S(2)}) copy-start(bf16[64,128]{1,0:T(8,128)(2,1)} %param.6) | copy-start | bytes 49156
  2.7 41.4 %all-to-all-start = ((bf16[4,1296,256]{2,1,0:T(8,128)(2,1)}), bf16[4,1296,256]{2,1,0:T(8,128)(2,1)S(1)}, u32[]{:S(2)}, u32[]{:S(2)}) async-start(bf16[4,1296,256]{2,1,0:T(8,128)(2,1)} %shard_map.55), calls=%async_computation | async-start | bytes 5308416 | tf_op jit(solution)/shard_map/all_to_all | solution.py:244
  106.7 4.6 %collective-permute-start = (bf16[16,64,512]{2,1,0:T(8,128)(2,1)S(1)}, bf16[16,64,512]{2,1,0:T(8,128)(2,1)S(1)}, u32[]{:S(2)}, u32[]{:S(2)}) collective-permute-start(bf16[16,64,512]{2,1,0:T(8,128)(2,1)S(1)} %shard_map.58), channel_id=1, source_target_pairs={{0,1},{1,0},{2,3},{3,2},{4,5},{5,4},{6,7},{7,6},{8,9},{9,8},{10,11... | collective-permute-start | bytes 3145736 | tf_op jit(solution)/shard_map/ppermute | solution.py:292

commit v5 on v4

--- a/solution.py
+++ b/solution.py
@@ -115,16 +115,27 @@
                 marks = jnp.where(lane == 2 * GROUP + g, rest, marks)
         out_ref[slot, :, GROUP * HD :] = marks.astype(jnp.bfloat16)
 
-    for ahead in range(NY):
-        seen = at_y + ahead < NY
+    low = at_z < NZ // 2
+    cases = [
+        (0, low, [0, 1]),
+        (0, jnp.logical_not(low), [0, 1, 2, 3]),
+        (1, at_y >= 0, [0, 1, 2, 3]),
+        (2, low, [0, 1, 2, 3]),
+        (2, jnp.logical_not(low), [1, 2, 3]),
+        (3, at_z == 0, [3]),
+    ]
+    for ahead, when, chunks in cases:
+
+        @pl.when((at_y + ahead < NY) & when)
+        def _(ahead=ahead, chunks=chunks):
+            band(ahead, chunks)
+
+    for ahead in range(1, NY):
+        unseen = at_y + ahead >= NY
         if ahead == 3:
-            seen = seen & (at_z == 0)
-
-        @pl.when(seen)
-        def _(ahead=ahead):
-            band(ahead, list(range(CHUNKS)) if ahead < 3 else [CHUNKS - 1])
-
-        @pl.when(jnp.logical_not(seen))
+            unseen = unseen | (at_z != 0)
+
+        @pl.when(unseen)
         def _(ahead=ahead):
             slot = (at_y + ahead + NY - at_z % NY) % NY
             out_ref[slot, :, : GROUP * HD] = jnp.zeros((TOK, GROUP * HD), jnp.bfloat16)
@@ -168,9 +179,13 @@
         for j in range(2):
             across = slice(j * width, (j + 1) * width)
             half_part = part[:, j]
-            if own:
-                half_part += refs[0][spot, :, across].astype(jnp.float32)
-            out_ref[spot, :, across] = half_part.astype(jnp.bfloat16)
+            out_ref[spot, :, across] = half_part.astype(out_ref.dtype)
+
+
+def add(own_ref, added_ref, out_ref):
+    for place in range(NY * NX):
+        total = own_ref[place] + added_ref[place].astype(jnp.float32)
+        out_ref[place] = total.astype(jnp.bfloat16)
 
 
 def combine(parts_ref, out_ref):
@@ -277,7 +292,9 @@
     def projected(own, *operands):
         return pl.pallas_call(
             functools.partial(project, own),
-            out_shape=jax.ShapeDtypeStruct((NY * NX, TOK, 2 * width), jnp.bfloat16),
+            out_shape=jax.ShapeDtypeStruct(
+                (NY * NX, TOK, 2 * width), jnp.float32 if own else jnp.bfloat16
+            ),
             in_specs=[VMEM] * (1 + len(operands)),
             out_specs=VMEM,
             scratch_shapes=[pltpu.VMEM((PLANE // 2, GROUP * HD), jnp.bfloat16)],
@@ -290,7 +307,13 @@
         )(rows, *operands)
 
     theirs = lax.ppermute(projected(False, sent), "tp", CORE_SWAP)
-    sums = projected(True, sent, theirs)
+    sums = pl.pallas_call(
+        add,
+        out_shape=jax.ShapeDtypeStruct((NY * NX, TOK, 2 * width), jnp.bfloat16),
+        in_specs=[VMEM] * 2,
+        out_specs=VMEM,
+        compiler_params=pltpu.CompilerParams(vmem_limit_bytes=16 * 1024 * 1024),
+    )(projected(True, sent), theirs)
     parts = lax.all_to_all(
         sums, ("seq", "tp"), 0, 0, axis_index_groups=PLANE_GROUPS, tiled=True
     )

time: 136 us -> 135 us (level)
  transfers between devices with their start and end apart: 2 -> 2, of which waited for: 1 -> 1; matrix products, arithmetic and copies ran while one was open for 0% -> 0% of each run, Pallas kernels for 0% -> 1%
where the time goes in v5:
time: 135 us; the launch traced here: 134 us
  blocking collectives  116 us (86%)
  Pallas kernels  9.92 us (7%)
  starting transfers between devices  6.53 us (5%)
  waiting for transfers between devices  1.37 us (1%)
    all_gather x1, blocking collectives, body(): lax.all_gather(attended.astype(jnp.float16), 'seq', axis_index_groups=Z_G...  44.8 us
    all_gather x1, blocking collectives, body(): plane = lax.all_gather(message, 'seq', axis_index_groups=Z_GROUPS)  36.7 us
    all_to_all x1, blocking collectives, body(): lax.all_to_all(sums, ('seq', 'tp'), 0, 0, axis_index_groups=PLANE_GROUPS,...  22.3 us
    all_to_all x1, blocking collectives, body(): lax.all_to_all(parts, 'seq', 0, 0, axis_index_groups=Y_GROUPS, tiled=True)  12 us
    all_to_all x1, starting transfers between devices, body(): lax.all_to_all(copies, 'seq', 0, 0, axis_index_groups=Y_GROUPS, tiled=True)  4.61 us
    pallas_call x1, Pallas kernels, body(): pl.pallas_call(attend, out_shape=jax.ShapeDtypeStruct((NY, TOK, WIDE), jn...  3.31 us
  transfers between devices with their start and end apart: 2, of which 1 were waited for; matrix products, arithmetic and copies ran while one was open for 0% of the time, Pallas kernels for 1%

profile of v5, /device:TPU:32, one launch (start us, length us, event | category | flops | bytes accessed | tf_op | source)
XLA Modules:
  0.0 134.4 jit_solution(15241171313902547961)
XLA Ops:
  0.0 2.6 %shard_map.55 = bf16[4,1296,256]{2,1,0:T(8,128)(2,1)} custom-call(bf16[1024,256]{1,0:T(8,128)(2,1)} %weight_ref.1, bf16[64,1024]{1,0:T(8,128)(2,1)} %q_ref.1, s32[1,64]{1,0:T(1,128)} %bitcast.5), custom_call_target="tpu_custom_call" | custom-call | tf_op jit(solution)/shard_map/pallas_call | solution.py:246
  2.6 0.0 copy-start.2
  2.6 0.0 copy-start
  2.6 0.0 copy-start.1
  2.7 4.6 %all-to-all-start = ((bf16[4,1296,256]{2,1,0:T(8,128)(2,1)}), bf16[4,1296,256]{2,1,0:T(8,128)(2,1)S(1)}, u32[]{:S(2)}, u32[]{:S(2)}) async-start(bf16[4,1296,256]{2,1,0:T(8,128)(2,1)} %shard_map.55), calls=%async_computation | async-start | bytes 5308416 | tf_op jit(solution)/shard_map/all_to_all | solution.py:259
  7.3 0.0 copy-done.2
  7.3 0.1 maximum_bitcast_fusion
  7.4 0.0 copy-done
  7.4 0.0 copy-done.1
  7.4 36.7 %all-gather = bf16[2304,128]{1,0:T(8,128)(2,1)S(1)} all-gather(bf16[144,128]{1,0:T(8,128)(2,1)S(1)} %fusion.1), channel_id=2, replica_groups={{0,8,16,24,32,40,48,56,64,72,80,88,96,104,112,120},{128,136,144,152,160..., dimensions={0}, use_global_device_ids=true | all-gather | bytes 626688 | tf_op jit(solution)/shard_map/all_gather | solution.py:264
  44.0 0.0 all-to-all-done.sent_ref.weight_ref
  44.0 3.3 %shard_map.56 = bf16[4,64,1152]{2,1,0:T(8,128)(2,1)S(1)} custom-call(bf16[4,1296,256]{2,1,0:T(8,128)(2,1)S(1)} %all-to-all-done.sent_ref.weight_ref, bf16[16,144,128]{2,1,0:T(8,128)(2,1)S(1)} %bitcast.4), custom_call_target="tpu_custom_call" | custom-call | flops 805306368 | bytes 3145728 | tf_op jit(solution)/shard_map/pallas_call | solution.py:266
  47.4 12.0 %all_to_all.15.parts_ref = bf16[4,64,1152]{2,1,0:T(8,128)(2,1)S(1)} all-to-all(bf16[4,64,1152]{2,1,0:T(8,128)(2,1)S(1)} %shard_map.56), channel_id=1, replica_groups={{0,128,256,384},{8,136,264,392},{16,144,272,400},{24,152,280,408},{32,1..., dimensions={0} | all-to-all | bytes 1179648 | tf_op jit(solution)/shard_map/all_to_all | solution.py:279
  59.4 0.5 shard_map.57
  59.9 44.8 %all-gather.2 = f16[1024,1024]{1,0:T(8,128)(2,1)S(1)} all-gather(f16[64,1024]{1,0:T(8,128)(2,1)S(1)} %convert_element_type.7), channel_id=1, replica_groups={{0,8,16,24,32,40,48,56,64,72,80,88,96,104,112,120},{128,136,144,152,160..., dimensions={0}, use_global_device_ids=true | all-gather | bytes 2228224 | tf_op jit(solution)/shard_map/all_gather | solution.py:288
  104.7 0.6 convert_element_type.8.rows_ref
  105.3 1.3 shard_map.59
  106.6 1.9 %collective-permute-start = (bf16[16,64,512]{2,1,0:T(8,128)(2,1)S(1)}, bf16[16,64,512]{2,1,0:T(8,128)(2,1)S(1)}, u32[]{:S(2)}, u32[]{:S(2)}) collective-permute-start(bf16[16,64,512]{2,1,0:T(8,128)(2,1)S(1)} %shard_map.59), channel_id=1, source_target_pairs={{0,1},{1,0},{2,3},{3,2},{4,5},{5,4},{6,7},{7,6},{8,9},{9,8},{10,11... | collective-permute-start | bytes 3145736 | tf_op jit(solution)/shard_map/ppermute | solution.py:309
  108.5 1.3 shard_map.58.own_ref
  109.7 1.4 %collective-permute-done.added_ref = bf16[16,64,512]{2,1,0:T(8,128)(2,1)S(1)} collective-permute-done((bf16[16,64,512]{2,1,0:T(8,128)(2,1)S(1)}, bf16[16,64,512]{2,1,0:T(8,128)(2,1)S(1)}, u32[]{:S(2)}, u32[]{:S(2)}) %collective-permute-start) | collective-permute-done | bytes 1048608 | tf_op jit(solution)/shard_map/ppermute | solution.py:309
  111.1 0.2 shard_map.60
  111.3 22.3 %all_to_all.16.parts_ref = bf16[16,64,512]{2,1,0:T(8,128)(2,1)S(1)} all-to-all(bf16[16,64,512]{2,1,0:T(8,128)(2,1)S(1)} %shard_map.60), channel_id=1, replica_groups={{0,2,4,6,128,130,132,134,256,258,260,262,384,386,388,390},{1,3,5,7,129,..., dimensions={0} | all-to-all | bytes 2097152 | tf_op jit(solution)/shard_map/all_to_all | solution.py:317
  133.5 0.8 shard_map.61
  (3 shorter events, 0.0 us)
Async XLA Ops:
  2.6 4.6 %copy-start.2 = (s32[64]{0:T(128)S(1)}, s32[64]{0:T(128)}, u32[]{:S(2)}) copy-start(s32[64]{0:T(128)} %param.8) | copy-start | bytes 772
  2.6 4.7 %copy-start = (bf16[64,128]{1,0:T(8,128)(2,1)S(1)}, bf16[64,128]{1,0:T(8,128)(2,1)}, u32[]{:S(2)}) copy-start(bf16[64,128]{1,0:T(8,128)(2,1)} %param.7) | copy-start | bytes 49156
  2.6 4.7 %copy-start.1 = (bf16[64,128]{1,0:T(8,128)(2,1)S(1)}, bf16[64,128]{1,0:T(8,128)(2,1)}, u32[]{:S(2)}) copy-start(bf16[64,128]{1,0:T(8,128)(2,1)} %param.6) | copy-start | bytes 49156
  2.7 41.4 %all-to-all-start = ((bf16[4,1296,256]{2,1,0:T(8,128)(2,1)}), bf16[4,1296,256]{2,1,0:T(8,128)(2,1)S(1)}, u32[]{:S(2)}, u32[]{:S(2)}) async-start(bf16[4,1296,256]{2,1,0:T(8,128)(2,1)} %shard_map.55), calls=%async_computation | async-start | bytes 5308416 | tf_op jit(solution)/shard_map/all_to_all | solution.py:259
  106.6 4.6 %collective-permute-start = (bf16[16,64,512]{2,1,0:T(8,128)(2,1)S(1)}, bf16[16,64,512]{2,1,0:T(8,128)(2,1)S(1)}, u32[]{:S(2)}, u32[]{:S(2)}) collective-permute-start(bf16[16,64,512]{2,1,0:T(8,128)(2,1)S(1)} %shard_map.59), channel_id=1, source_target_pairs={{0,1},{1,0},{2,3},{3,2},{4,5},{5,4},{6,7},{7,6},{8,9},{9,8},{10,11... | collective-permute-start | bytes 3145736 | tf_op jit(solution)/shard_map/ppermute | solution.py:309

commit v6 on v5

--- a/solution.py
+++ b/solution.py
@@ -17,6 +17,7 @@
 HEADS_AT_ONCE = 4
 PLANE = NZ * TOK
 SEG_ROWS = 16
+PIECES = 4
 WEIGHT_ROWS = GROUP * HD
 QUERY_ROWS = GROUP * TOK // 2
 SENT_ROWS = WEIGHT_ROWS + QUERY_ROWS + SEG_ROWS
@@ -35,7 +36,7 @@
 
 
 PLANE_GROUPS = [
-    [flat(y, z, x, c) for y in range(NY) for x in range(NX)] for z in range(NZ) for c in range(NC)
+    [flat(y, z, x, c) for x in range(NX) for y in range(NY)] for z in range(NZ) for c in range(NC)
 ]
 def attend(sent_ref, plane_ref, out_ref, score_ref):
     at_y, at_z = lax.axis_index("seq") // NZ, lax.axis_index("seq") % NZ
@@ -60,6 +61,8 @@
             [ids_of(plane_ref[4 * i + j, 2 * TOK :]) for j in range(4)], axis=1
         )
 
+    all_key_ids = [key_ids(i) for i in range(CHUNKS)]
+
     def band(ahead, chunks):
         y = at_y + ahead
         slot = (y + NY - at_z % NY) % NY
@@ -69,7 +72,7 @@
         values = [part_of(i, TOK) for i in chunks]
         keeps = []
         for i in chunks:
-            keep = key_ids(i) == own
+            keep = all_key_ids[i] == own
             if ahead == 0:
                 at = i * CHUNK + lax.broadcasted_iota(jnp.int32, (TOK, CHUNK), 1)
                 keep = keep & (at <= position)
@@ -171,15 +174,15 @@
             block = (2 * half + j) * 4 + (x + NY - at_y) % NY
             source = pl.ds(pl.multiple_of(block * TOK, TOK), TOK)
             picked_ref[pl.ds((2 * x + j) * TOK, TOK), :] = rows_ref[source, :]
-    for d in range(NY):
-        part = jnp.dot(picked_ref[...], weight_ref[d, :WEIGHT_ROWS], preferred_element_type=jnp.float32)
+    for y in range(NY):
+        part = jnp.dot(
+            picked_ref[...], weight_ref[y, :WEIGHT_ROWS], preferred_element_type=jnp.float32
+        )
         width = part.shape[-1]
-        part = part.reshape(NX, 2, TOK, width)
-        spot = pl.ds(d * NX, NX)
-        for j in range(2):
-            across = slice(j * width, (j + 1) * width)
-            half_part = part[:, j]
-            out_ref[spot, :, across] = half_part.astype(out_ref.dtype)
+        part = part.reshape(NX, 2, TOK, width).astype(out_ref.dtype)
+        for x in range(NX):
+            for j in range(2):
+                out_ref[x * NY + y, :, j * width : (j + 1) * width] = part[x, j]
 
 
 def add(own_ref, added_ref, out_ref):
@@ -192,9 +195,9 @@
     at_x = lax.axis_index("tp") // NC
     width = out_ref.shape[1]
     for y in range(NY):
-        total = parts_ref[y * NX].astype(jnp.float32)
+        total = parts_ref[y].astype(jnp.float32)
         for x in range(1, NX):
-            total += parts_ref[y * NX + x].astype(jnp.float32)
+            total += parts_ref[x * NY + y].astype(jnp.float32)
         total = total.astype(jnp.bfloat16)
         for j in range(2):
             block = 4 * j + (at_x + NY - y) % NY
@@ -204,19 +207,19 @@
 
 def spread(weight_ref, q_ref, ids_ref, out_ref, held_ref, own_ref, in_sems, out_sems):
     width = weight_ref.shape[1]
-    half = WEIGHT_ROWS // 2
+    size = WEIGHT_ROWS // PIECES
     arrivals = []
-    for piece in range(2):
-        part = pl.ds(piece * half, half)
+    for piece in range(PIECES):
+        part = pl.ds(piece * size, size)
         copy = pltpu.make_async_copy(weight_ref.at[part], held_ref.at[part], in_sems.at[piece])
         arrivals.append((part, [copy]))
     pieces = []
     for k in range(q_ref.shape[1] // width):
         target = held_ref.at[pl.ds(WEIGHT_ROWS + k * TOK, TOK)]
         source = q_ref.at[:, pl.ds(k * width, width)]
-        pieces.append(pltpu.make_async_copy(source, target, in_sems.at[2 + k]))
+        pieces.append(pltpu.make_async_copy(source, target, in_sems.at[PIECES + k]))
     arrivals.append((pl.ds(WEIGHT_ROWS, SENT_ROWS - WEIGHT_ROWS), pieces))
-    fetch = pltpu.make_async_copy(ids_ref, own_ref, in_sems.at[6])
+    fetch = pltpu.make_async_copy(ids_ref, own_ref, in_sems.at[PIECES + 4])
     fetch.start()
     for _, copies in arrivals:
         for copy in copies:
@@ -225,7 +228,7 @@
     for index, (part, copies) in enumerate(arrivals):
         for copy in copies:
             copy.wait()
-        if index == 2:
+        if index == PIECES:
             fetch.wait()
             ids = own_ref[...]
             both = jnp.concatenate([ids & 127, ids >> 7, ids & 0, ids & 0], axis=1)
@@ -251,8 +254,8 @@
         scratch_shapes=[
             pltpu.VMEM((SENT_ROWS, width), jnp.bfloat16),
             pltpu.VMEM((1, TOK), jnp.int32),
-            pltpu.SemaphoreType.DMA((7,)),
-            pltpu.SemaphoreType.DMA((3, NY)),
+            pltpu.SemaphoreType.DMA((PIECES + 5,)),
+            pltpu.SemaphoreType.DMA((PIECES + 1, NY)),
         ],
         compiler_params=pltpu.CompilerParams(vmem_limit_bytes=60 * 1024 * 1024),
     )(out_weight, queries, segment_ids.reshape(1, TOK))

time: 135 us -> 135 us (level)
  no operation moved by 1% of the time
where the time goes in v6:
time: 135 us; the launch traced here: 134 us
  blocking collectives  116 us (86%)
  Pallas kernels  10 us (7%)
  starting transfers between devices  6.53 us (5%)
  waiting for transfers between devices  1.37 us (1%)
    all_gather x1, blocking collectives, body(): lax.all_gather(attended.astype(jnp.float16), 'seq', axis_index_groups=Z_G...  44.8 us
    all_gather x1, blocking collectives, body(): plane = lax.all_gather(message, 'seq', axis_index_groups=Z_GROUPS)  36.7 us
    all_to_all x1, blocking collectives, body(): lax.all_to_all(sums, ('seq', 'tp'), 0, 0, axis_index_groups=PLANE_GROUPS,...  22.2 us
    all_to_all x1, blocking collectives, body(): lax.all_to_all(parts, 'seq', 0, 0, axis_index_groups=Y_GROUPS, tiled=True)  12 us
    all_to_all x1, starting transfers between devices, body(): lax.all_to_all(copies, 'seq', 0, 0, axis_index_groups=Y_GROUPS, tiled=True)  4.61 us
    pallas_call x1, Pallas kernels, body(): pl.pallas_call(attend, out_shape=jax.ShapeDtypeStruct((NY, TOK, WIDE), jn...  3.37 us
  transfers between devices with their start and end apart: 2, of which 1 were waited for; matrix products, arithmetic and copies ran while one was open for 0% of the time, Pallas kernels for 1%

profile of v6, /device:TPU:32, one launch (start us, length us, event | category | flops | bytes accessed | tf_op | source)
XLA Modules:
  0.0 134.5 jit_solution(1642606050017642425)
XLA Ops:
  0.0 2.7 %shard_map.55 = bf16[4,1296,256]{2,1,0:T(8,128)(2,1)} custom-call(bf16[1024,256]{1,0:T(8,128)(2,1)} %weight_ref.1, bf16[64,1024]{1,0:T(8,128)(2,1)} %q_ref.1, s32[1,64]{1,0:T(1,128)} %bitcast.5), custom_call_target="tpu_custom_call" | custom-call | tf_op jit(solution)/shard_map/pallas_call | solution.py:249
  2.7 0.0 copy-start.2
  2.7 0.0 copy-start
  2.7 0.0 copy-start.1
  2.7 4.6 %all-to-all-start = ((bf16[4,1296,256]{2,1,0:T(8,128)(2,1)}), bf16[4,1296,256]{2,1,0:T(8,128)(2,1)S(1)}, u32[]{:S(2)}, u32[]{:S(2)}) async-start(bf16[4,1296,256]{2,1,0:T(8,128)(2,1)} %shard_map.55), calls=%async_computation | async-start | bytes 5308416 | tf_op jit(solution)/shard_map/all_to_all | solution.py:262
  7.3 0.0 copy-done.2
  7.3 0.1 maximum_bitcast_fusion
  7.4 0.0 copy-done
  7.4 0.0 copy-done.1
  7.4 36.7 %all-gather = bf16[2304,128]{1,0:T(8,128)(2,1)S(1)} all-gather(bf16[144,128]{1,0:T(8,128)(2,1)S(1)} %fusion.1), channel_id=2, replica_groups={{0,8,16,24,32,40,48,56,64,72,80,88,96,104,112,120},{128,136,144,152,160..., dimensions={0}, use_global_device_ids=true | all-gather | bytes 626688 | tf_op jit(solution)/shard_map/all_gather | solution.py:267
  44.1 0.0 all-to-all-done.sent_ref.weight_ref
  44.1 3.4 %shard_map.56 = bf16[4,64,1152]{2,1,0:T(8,128)(2,1)S(1)} custom-call(bf16[4,1296,256]{2,1,0:T(8,128)(2,1)S(1)} %all-to-all-done.sent_ref.weight_ref, bf16[16,144,128]{2,1,0:T(8,128)(2,1)S(1)} %bitcast.4), custom_call_target="tpu_custom_call" | custom-call | flops 805306368 | bytes 3145728 | tf_op jit(solution)/shard_map/pallas_call | solution.py:269
  47.5 12.0 %all_to_all.15.parts_ref = bf16[4,64,1152]{2,1,0:T(8,128)(2,1)S(1)} all-to-all(bf16[4,64,1152]{2,1,0:T(8,128)(2,1)S(1)} %shard_map.56), channel_id=1, replica_groups={{0,128,256,384},{8,136,264,392},{16,144,272,400},{24,152,280,408},{32,1..., dimensions={0} | all-to-all | bytes 1179648 | tf_op jit(solution)/shard_map/all_to_all | solution.py:282
  59.5 0.5 shard_map.57
  60.0 44.8 %all-gather.2 = f16[1024,1024]{1,0:T(8,128)(2,1)S(1)} all-gather(f16[64,1024]{1,0:T(8,128)(2,1)S(1)} %convert_element_type.7), channel_id=1, replica_groups={{0,8,16,24,32,40,48,56,64,72,80,88,96,104,112,120},{128,136,144,152,160..., dimensions={0}, use_global_device_ids=true | all-gather | bytes 2228224 | tf_op jit(solution)/shard_map/all_gather | solution.py:291
  104.9 0.6 convert_element_type.8.rows_ref
  105.4 1.3 shard_map.59
  106.7 1.9 %collective-permute-start = (bf16[16,64,512]{2,1,0:T(8,128)(2,1)S(1)}, bf16[16,64,512]{2,1,0:T(8,128)(2,1)S(1)}, u32[]{:S(2)}, u32[]{:S(2)}) collective-permute-start(bf16[16,64,512]{2,1,0:T(8,128)(2,1)S(1)} %shard_map.59), channel_id=1, source_target_pairs={{0,1},{1,0},{2,3},{3,2},{4,5},{5,4},{6,7},{7,6},{8,9},{9,8},{10,11... | collective-permute-start | bytes 3145736 | tf_op jit(solution)/shard_map/ppermute | solution.py:312
  108.6 1.3 shard_map.58.own_ref
  109.9 1.4 %collective-permute-done.added_ref = bf16[16,64,512]{2,1,0:T(8,128)(2,1)S(1)} collective-permute-done((bf16[16,64,512]{2,1,0:T(8,128)(2,1)S(1)}, bf16[16,64,512]{2,1,0:T(8,128)(2,1)S(1)}, u32[]{:S(2)}, u32[]{:S(2)}) %collective-permute-start) | collective-permute-done | bytes 1048608 | tf_op jit(solution)/shard_map/ppermute | solution.py:312
  111.3 0.2 shard_map.60
  111.4 22.2 %all_to_all.16.parts_ref = bf16[16,64,512]{2,1,0:T(8,128)(2,1)S(1)} all-to-all(bf16[16,64,512]{2,1,0:T(8,128)(2,1)S(1)} %shard_map.60), channel_id=1, replica_groups={{0,128,256,384,2,130,258,386,4,132,260,388,6,134,262,390},{1,129,257,38..., dimensions={0} | all-to-all | bytes 2097152 | tf_op jit(solution)/shard_map/all_to_all | solution.py:320
  133.7 0.8 shard_map.61
  (3 shorter events, 0.0 us)
Async XLA Ops:
  2.7 4.6 %copy-start.2 = (s32[64]{0:T(128)S(1)}, s32[64]{0:T(128)}, u32[]{:S(2)}) copy-start(s32[64]{0:T(128)} %param.8) | copy-start | bytes 772
  2.7 4.7 %copy-start = (bf16[64,128]{1,0:T(8,128)(2,1)S(1)}, bf16[64,128]{1,0:T(8,128)(2,1)}, u32[]{:S(2)}) copy-start(bf16[64,128]{1,0:T(8,128)(2,1)} %param.7) | copy-start | bytes 49156
  2.7 4.7 %copy-start.1 = (bf16[64,128]{1,0:T(8,128)(2,1)S(1)}, bf16[64,128]{1,0:T(8,128)(2,1)}, u32[]{:S(2)}) copy-start(bf16[64,128]{1,0:T(8,128)(2,1)} %param.6) | copy-start | bytes 49156
  2.7 41.4 %all-to-all-start = ((bf16[4,1296,256]{2,1,0:T(8,128)(2,1)}), bf16[4,1296,256]{2,1,0:T(8,128)(2,1)S(1)}, u32[]{:S(2)}, u32[]{:S(2)}) async-start(bf16[4,1296,256]{2,1,0:T(8,128)(2,1)} %shard_map.55), calls=%async_computation | async-start | bytes 5308416 | tf_op jit(solution)/shard_map/all_to_all | solution.py:262
  106.7 4.6 %collective-permute-start = (bf16[16,64,512]{2,1,0:T(8,128)(2,1)S(1)}, bf16[16,64,512]{2,1,0:T(8,128)(2,1)S(1)}, u32[]{:S(2)}, u32[]{:S(2)}) collective-permute-start(bf16[16,64,512]{2,1,0:T(8,128)(2,1)S(1)} %shard_map.59), channel_id=1, source_target_pairs={{0,1},{1,0},{2,3},{3,2},{4,5},{5,4},{6,7},{7,6},{8,9},{9,8},{10,11... | collective-permute-start | bytes 3145736 | tf_op jit(solution)/shard_map/ppermute | solution.py:312

commit v7 on v6

--- a/solution.py
+++ b/solution.py
@@ -17,7 +17,6 @@
 HEADS_AT_ONCE = 4
 PLANE = NZ * TOK
 SEG_ROWS = 16
-PIECES = 4
 WEIGHT_ROWS = GROUP * HD
 QUERY_ROWS = GROUP * TOK // 2
 SENT_ROWS = WEIGHT_ROWS + QUERY_ROWS + SEG_ROWS
@@ -61,8 +60,6 @@
             [ids_of(plane_ref[4 * i + j, 2 * TOK :]) for j in range(4)], axis=1
         )
 
-    all_key_ids = [key_ids(i) for i in range(CHUNKS)]
-
     def band(ahead, chunks):
         y = at_y + ahead
         slot = (y + NY - at_z % NY) % NY
@@ -72,7 +69,7 @@
         values = [part_of(i, TOK) for i in chunks]
         keeps = []
         for i in chunks:
-            keep = all_key_ids[i] == own
+            keep = key_ids(i) == own
             if ahead == 0:
                 at = i * CHUNK + lax.broadcasted_iota(jnp.int32, (TOK, CHUNK), 1)
                 keep = keep & (at <= position)
@@ -207,19 +204,19 @@
 
 def spread(weight_ref, q_ref, ids_ref, out_ref, held_ref, own_ref, in_sems, out_sems):
     width = weight_ref.shape[1]
-    size = WEIGHT_ROWS // PIECES
+    half = WEIGHT_ROWS // 2
     arrivals = []
-    for piece in range(PIECES):
-        part = pl.ds(piece * size, size)
+    for piece in range(2):
+        part = pl.ds(piece * half, half)
         copy = pltpu.make_async_copy(weight_ref.at[part], held_ref.at[part], in_sems.at[piece])
         arrivals.append((part, [copy]))
     pieces = []
     for k in range(q_ref.shape[1] // width):
         target = held_ref.at[pl.ds(WEIGHT_ROWS + k * TOK, TOK)]
         source = q_ref.at[:, pl.ds(k * width, width)]
-        pieces.append(pltpu.make_async_copy(source, target, in_sems.at[PIECES + k]))
+        pieces.append(pltpu.make_async_copy(source, target, in_sems.at[2 + k]))
     arrivals.append((pl.ds(WEIGHT_ROWS, SENT_ROWS - WEIGHT_ROWS), pieces))
-    fetch = pltpu.make_async_copy(ids_ref, own_ref, in_sems.at[PIECES + 4])
+    fetch = pltpu.make_async_copy(ids_ref, own_ref, in_sems.at[6])
     fetch.start()
     for _, copies in arrivals:
         for copy in copies:
@@ -228,7 +225,7 @@
     for index, (part, copies) in enumerate(arrivals):
         for copy in copies:
             copy.wait()
-        if index == PIECES:
+        if index == 2:
             fetch.wait()
             ids = own_ref[...]
             both = jnp.concatenate([ids & 127, ids >> 7, ids & 0, ids & 0], axis=1)
@@ -254,8 +251,8 @@
         scratch_shapes=[
             pltpu.VMEM((SENT_ROWS, width), jnp.bfloat16),
             pltpu.VMEM((1, TOK), jnp.int32),
-            pltpu.SemaphoreType.DMA((PIECES + 5,)),
-            pltpu.SemaphoreType.DMA((PIECES + 1, NY)),
+            pltpu.SemaphoreType.DMA((7,)),
+            pltpu.SemaphoreType.DMA((3, NY)),
         ],
         compiler_params=pltpu.CompilerParams(vmem_limit_bytes=60 * 1024 * 1024),
     )(out_weight, queries, segment_ids.reshape(1, TOK))

time: 135 us -> 135 us (level)
  no operation moved by 1% of the time
where the time goes in v7:
time: 135 us; the launch traced here: 134 us
  blocking collectives  116 us (86%)
  Pallas kernels  9.92 us (7%)
  starting transfers between devices  6.53 us (5%)
  waiting for transfers between devices  1.37 us (1%)
    all_gather x1, blocking collectives, body(): lax.all_gather(attended.astype(jnp.float16), 'seq', axis_index_groups=Z_G...  44.8 us
    all_gather x1, blocking collectives, body(): plane = lax.all_gather(message, 'seq', axis_index_groups=Z_GROUPS)  36.7 us
    all_to_all x1, blocking collectives, body(): lax.all_to_all(sums, ('seq', 'tp'), 0, 0, axis_index_groups=PLANE_GROUPS,...  22.2 us
    all_to_all x1, blocking collectives, body(): lax.all_to_all(parts, 'seq', 0, 0, axis_index_groups=Y_GROUPS, tiled=True)  12 us
    all_to_all x1, starting transfers between devices, body(): lax.all_to_all(copies, 'seq', 0, 0, axis_index_groups=Y_GROUPS, tiled=True)  4.61 us
    pallas_call x1, Pallas kernels, body(): pl.pallas_call(attend, out_shape=jax.ShapeDtypeStruct((NY, TOK, WIDE), jn...  3.31 us
  transfers between devices with their start and end apart: 2, of which 1 were waited for; matrix products, arithmetic and copies ran while one was open for 0% of the time, Pallas kernels for 1%

profile of v7, /device:TPU:32, one launch (start us, length us, event | category | flops | bytes accessed | tf_op | source)
XLA Modules:
  0.0 134.3 jit_solution(356275425845778420)
XLA Ops:
  0.0 2.6 %shard_map.55 = bf16[4,1296,256]{2,1,0:T(8,128)(2,1)} custom-call(bf16[1024,256]{1,0:T(8,128)(2,1)} %weight_ref.1, bf16[64,1024]{1,0:T(8,128)(2,1)} %q_ref.1, s32[1,64]{1,0:T(1,128)} %bitcast.5), custom_call_target="tpu_custom_call" | custom-call | tf_op jit(solution)/shard_map/pallas_call | solution.py:246
  2.6 0.0 copy-start.2
  2.6 0.0 copy-start
  2.6 0.0 copy-start.1
  2.7 4.6 %all-to-all-start = ((bf16[4,1296,256]{2,1,0:T(8,128)(2,1)}), bf16[4,1296,256]{2,1,0:T(8,128)(2,1)S(1)}, u32[]{:S(2)}, u32[]{:S(2)}) async-start(bf16[4,1296,256]{2,1,0:T(8,128)(2,1)} %shard_map.55), calls=%async_computation | async-start | bytes 5308416 | tf_op jit(solution)/shard_map/all_to_all | solution.py:259
  7.3 0.0 copy-done.2
  7.3 0.1 maximum_bitcast_fusion
  7.4 0.0 copy-done
  7.4 0.0 copy-done.1
  7.4 36.7 %all-gather = bf16[2304,128]{1,0:T(8,128)(2,1)S(1)} all-gather(bf16[144,128]{1,0:T(8,128)(2,1)S(1)} %fusion.1), channel_id=2, replica_groups={{0,8,16,24,32,40,48,56,64,72,80,88,96,104,112,120},{128,136,144,152,160..., dimensions={0}, use_global_device_ids=true | all-gather | bytes 626688 | tf_op jit(solution)/shard_map/all_gather | solution.py:264
  44.0 0.0 all-to-all-done.sent_ref.weight_ref
  44.0 3.3 %shard_map.56 = bf16[4,64,1152]{2,1,0:T(8,128)(2,1)S(1)} custom-call(bf16[4,1296,256]{2,1,0:T(8,128)(2,1)S(1)} %all-to-all-done.sent_ref.weight_ref, bf16[16,144,128]{2,1,0:T(8,128)(2,1)S(1)} %bitcast.4), custom_call_target="tpu_custom_call" | custom-call | flops 805306368 | bytes 3145728 | tf_op jit(solution)/shard_map/pallas_call | solution.py:266
  47.4 12.0 %all_to_all.15.parts_ref = bf16[4,64,1152]{2,1,0:T(8,128)(2,1)S(1)} all-to-all(bf16[4,64,1152]{2,1,0:T(8,128)(2,1)S(1)} %shard_map.56), channel_id=1, replica_groups={{0,128,256,384},{8,136,264,392},{16,144,272,400},{24,152,280,408},{32,1..., dimensions={0} | all-to-all | bytes 1179648 | tf_op jit(solution)/shard_map/all_to_all | solution.py:279
  59.4 0.5 shard_map.57
  59.9 44.8 %all-gather.2 = f16[1024,1024]{1,0:T(8,128)(2,1)S(1)} all-gather(f16[64,1024]{1,0:T(8,128)(2,1)S(1)} %convert_element_type.7), channel_id=1, replica_groups={{0,8,16,24,32,40,48,56,64,72,80,88,96,104,112,120},{128,136,144,152,160..., dimensions={0}, use_global_device_ids=true | all-gather | bytes 2228224 | tf_op jit(solution)/shard_map/all_gather | solution.py:288
  104.7 0.6 convert_element_type.8.rows_ref
  105.3 1.3 shard_map.59
  106.6 1.9 %collective-permute-start = (bf16[16,64,512]{2,1,0:T(8,128)(2,1)S(1)}, bf16[16,64,512]{2,1,0:T(8,128)(2,1)S(1)}, u32[]{:S(2)}, u32[]{:S(2)}) collective-permute-start(bf16[16,64,512]{2,1,0:T(8,128)(2,1)S(1)} %shard_map.59), channel_id=1, source_target_pairs={{0,1},{1,0},{2,3},{3,2},{4,5},{5,4},{6,7},{7,6},{8,9},{9,8},{10,11... | collective-permute-start | bytes 3145736 | tf_op jit(solution)/shard_map/ppermute | solution.py:309
  108.5 1.3 shard_map.58.own_ref
  109.7 1.4 %collective-permute-done.added_ref = bf16[16,64,512]{2,1,0:T(8,128)(2,1)S(1)} collective-permute-done((bf16[16,64,512]{2,1,0:T(8,128)(2,1)S(1)}, bf16[16,64,512]{2,1,0:T(8,128)(2,1)S(1)}, u32[]{:S(2)}, u32[]{:S(2)}) %collective-permute-start) | collective-permute-done | bytes 1048608 | tf_op jit(solution)/shard_map/ppermute | solution.py:309
  111.1 0.2 shard_map.60
  111.3 22.2 %all_to_all.16.parts_ref = bf16[16,64,512]{2,1,0:T(8,128)(2,1)S(1)} all-to-all(bf16[16,64,512]{2,1,0:T(8,128)(2,1)S(1)} %shard_map.60), channel_id=1, replica_groups={{0,128,256,384,2,130,258,386,4,132,260,388,6,134,262,390},{1,129,257,38..., dimensions={0} | all-to-all | bytes 2097152 | tf_op jit(solution)/shard_map/all_to_all | solution.py:317
  133.5 0.8 shard_map.61
  (3 shorter events, 0.0 us)
Async XLA Ops:
  2.6 4.6 %copy-start.2 = (s32[64]{0:T(128)S(1)}, s32[64]{0:T(128)}, u32[]{:S(2)}) copy-start(s32[64]{0:T(128)} %param.8) | copy-start | bytes 772
  2.6 4.7 %copy-start = (bf16[64,128]{1,0:T(8,128)(2,1)S(1)}, bf16[64,128]{1,0:T(8,128)(2,1)}, u32[]{:S(2)}) copy-start(bf16[64,128]{1,0:T(8,128)(2,1)} %param.7) | copy-start | bytes 49156
  2.6 4.7 %copy-start.1 = (bf16[64,128]{1,0:T(8,128)(2,1)S(1)}, bf16[64,128]{1,0:T(8,128)(2,1)}, u32[]{:S(2)}) copy-start(bf16[64,128]{1,0:T(8,128)(2,1)} %param.6) | copy-start | bytes 49156
  2.7 41.4 %all-to-all-start = ((bf16[4,1296,256]{2,1,0:T(8,128)(2,1)}), bf16[4,1296,256]{2,1,0:T(8,128)(2,1)S(1)}, u32[]{:S(2)}, u32[]{:S(2)}) async-start(bf16[4,1296,256]{2,1,0:T(8,128)(2,1)} %shard_map.55), calls=%async_computation | async-start | bytes 5308416 | tf_op jit(solution)/shard_map/all_to_all | solution.py:259
  106.6 4.6 %collective-permute-start = (bf16[16,64,512]{2,1,0:T(8,128)(2,1)S(1)}, bf16[16,64,512]{2,1,0:T(8,128)(2,1)S(1)}, u32[]{:S(2)}, u32[]{:S(2)}) collective-permute-start(bf16[16,64,512]{2,1,0:T(8,128)(2,1)S(1)} %shard_map.59), channel_id=1, source_target_pairs={{0,1},{1,0},{2,3},{3,2},{4,5},{5,4},{6,7},{7,6},{8,9},{9,8},{10,11... | collective-permute-start | bytes 3145736 | tf_op jit(solution)/shard_map/ppermute | solution.py:309
